TPU v7x, 128 devices: a whole 4x4x4 slice. The times are simulated.
128 devices in a mesh: group: 8 (over z, core), member: 16 (over x, y).
Axes of the slice: x: 4, y: 4, z: 4, core: 2. Of those that a mesh axis runs over, the one named last changes fastest.
Arguments:
- query_feat: bfloat16 [16384, 4096], P(('group', 'member'))
- code_feat: bfloat16 [16384, 4096], P(('group', 'member'))
- projection: bfloat16 [4096, 1024], replicated
- hard_ids: int32 [128, 16], P(('group', 'member')), may hold values from 0 to 255, as said below
- loss_weight: float32 [16384], P(('group', 'member')), may hold values from 1 to 4
Outputs:
- query_grad: bfloat16 [16384, 4096], P(('group', 'member'))
- code_grad: bfloat16 [16384, 4096], P(('group', 'member'))
- projection_grad: float32 [4096, 1024], P(('group', 'member'))
Inputs may be any that keep to these rules, and one draw needn't show every extreme that they name: `hard_ids`: entry (owner device g * 16 + m) * 2 + slot names code rows of that device. A row names 16 different blocks, none of its own group; at most 4 of them lie in one group, and exactly 4 in some group of every row.
All inputs are finite; a program needn't handle non-finite values.
Results may differ from a plain program's by a relative error of at most 0.02.
Values may be sent and summed in bfloat16 or wider, within the bound.
A program may use at most 128 MiB of HBM per device.

v0:
```python
import jax
import jax.numpy as jnp
from jax import lax
from jax.sharding import PartitionSpec as P

CB = 64


inverse_temp = 120.0
epsilon = 1e-06


def embed(features, projection):
    values = jnp.dot(features, projection, preferred_element_type=jnp.float32)
    inverse = lax.rsqrt(jnp.sum(values * values, axis=1) + epsilon)
    unit_vec = values * inverse[:, None]
    return (unit_vec, inverse, unit_vec.astype(jnp.bfloat16))


def norm_back(upstream, unit_vec, inverse):
    inner_prod = jnp.sum(unit_vec * upstream, axis=1, keepdims=True)
    return (inverse[:, None] * (upstream - unit_vec * inner_prod)).astype(jnp.bfloat16)


def body(query_feat, code_feat, projection, hard_ids, loss_weight):
    groups = lax.axis_size("group")
    members = lax.axis_size("member")
    member_index = lax.axis_index("member")
    queries_dev = query_feat.shape[0]
    emb_width = projection.shape[1]
    count_hard = hard_ids.shape[1]
    slot_count = queries_dev // CB
    per_group = members * slot_count
    capacity = 2 * count_hard // groups
    q_unit, q_inv, q_emb = embed(query_feat, projection)
    c_unit, c_inv, c_emb = embed(code_feat, projection)
    group_codes = lax.all_gather(c_emb, "member", axis=0, tiled=True)
    code_blocks = group_codes.reshape(per_group, CB, emb_width)
    wanted = hard_ids[0]
    owner_group = wanted // per_group
    local_block = wanted % per_group
    request_order = jnp.arange(count_hard, dtype=jnp.int32)
    same_group = (owner_group[:, None] == owner_group[None, :]) & (
        request_order[None, :] < request_order[:, None]
    )
    slot_place = jnp.sum(same_group.astype(jnp.int32), axis=1)
    pick_group = (owner_group[:, None] == jnp.arange(groups, dtype=jnp.int32)[None, :]).astype(
        jnp.int32
    )
    pick_place = (slot_place[:, None] == jnp.arange(capacity, dtype=jnp.int32)[None, :]).astype(
        jnp.int32
    )
    request_table = (
        jnp.sum(
            pick_group[:, :, None] * (pick_place * (local_block + 1)[:, None])[:, None, :], axis=0
        )
        - 1
    )
    asked_blocks = lax.all_to_all(request_table, "group", split_axis=0, concat_axis=0, tiled=True)
    asked_valid = asked_blocks >= 0
    picked = (
        code_blocks[jnp.clip(asked_blocks, 0, per_group - 1)]
        * asked_valid.astype(jnp.bfloat16)[:, :, None, None]
    )
    group_scores = inverse_temp * jnp.einsum(
        "qe,ke->qk", q_emb, group_codes, preferred_element_type=jnp.float32
    )
    offsets = jnp.arange(queries_dev, dtype=jnp.int32)
    columns = jnp.arange(members * queries_dev, dtype=jnp.int32)
    positive = (columns[None, :] == (member_index * queries_dev + offsets)[:, None]).astype(
        jnp.float32
    )
    factor = loss_weight * inverse_temp
    fetched = lax.all_to_all(picked, "group", split_axis=0, concat_axis=0, tiled=True).reshape(
        groups * capacity * CB, emb_width
    )
    table_valid = jnp.broadcast_to(
        (request_table >= 0)[:, :, None], (groups, capacity, CB)
    ).reshape(-1)
    hard_scores = jnp.where(
        table_valid[None, :],
        inverse_temp * jnp.einsum("qe,ke->qk", q_emb, fetched, preferred_element_type=jnp.float32),
        -jnp.inf,
    )
    row_max = jnp.maximum(jnp.max(group_scores, axis=1), jnp.max(hard_scores, axis=1))
    row_sum = jnp.sum(jnp.exp(group_scores - row_max[:, None]), axis=1) + jnp.sum(
        jnp.exp(hard_scores - row_max[:, None]), axis=1
    )
    log_total = row_max + jnp.log(row_sum)
    grad_hard = (factor[:, None] * jnp.exp(hard_scores - log_total[:, None])).astype(jnp.bfloat16)
    hard_delta = jnp.einsum("qk,ke->qe", grad_hard, fetched, preferred_element_type=jnp.float32)
    outgoing = jnp.einsum("qk,qe->ke", grad_hard, q_emb, preferred_element_type=jnp.float32).astype(
        jnp.bfloat16
    )
    returned = lax.all_to_all(
        outgoing.reshape(groups, capacity, CB, emb_width),
        "group",
        split_axis=0,
        concat_axis=0,
        tiled=True,
    )
    grad_group = (factor[:, None] * (jnp.exp(group_scores - log_total[:, None]) - positive)).astype(
        jnp.bfloat16
    )
    query_delta = (
        jnp.einsum("qk,ke->qe", grad_group, group_codes, preferred_element_type=jnp.float32)
        + hard_delta
    )
    hit_table = (
        asked_blocks.reshape(-1)[:, None] == jnp.arange(per_group, dtype=jnp.int32)[None, :]
    ).astype(jnp.bfloat16)
    hard_sum = jnp.einsum(
        "rj,rx->jx",
        hit_table,
        returned.reshape(groups * capacity, CB * emb_width),
        preferred_element_type=jnp.float32,
    )
    code_terms = jnp.einsum(
        "qk,qe->ke", grad_group, q_emb, preferred_element_type=jnp.float32
    ) + hard_sum.reshape(members * queries_dev, emb_width)
    code_delta = lax.psum_scatter(
        code_terms.astype(jnp.bfloat16), "member", scatter_dimension=0, tiled=True
    ).astype(jnp.float32)
    dz_query = norm_back(query_delta, q_unit, q_inv)
    dz_code = norm_back(code_delta, c_unit, c_inv)
    query_grad = jnp.einsum(
        "qe,de->qd", dz_query, projection, preferred_element_type=jnp.float32
    ).astype(jnp.bfloat16)
    code_grad = jnp.einsum(
        "qe,de->qd", dz_code, projection, preferred_element_type=jnp.float32
    ).astype(jnp.bfloat16)
    projection_grad = lax.psum_scatter(
        jnp.einsum("qd,qe->de", query_feat, dz_query, preferred_element_type=jnp.float32)
        + jnp.einsum("qd,qe->de", code_feat, dz_code, preferred_element_type=jnp.float32),
        ("group", "member"),
        scatter_dimension=0,
        tiled=True,
    )
    return (query_grad, code_grad, projection_grad)


def solution(mesh):
    return jax.shard_map(
        body,
        mesh=mesh,
        in_specs=(
            P(("group", "member"), None),
            P(("group", "member"), None),
            P(),
            P(("group", "member"), None),
            P(("group", "member")),
        ),
        out_specs=(
            P(("group", "member"), None),
            P(("group", "member"), None),
            P(("group", "member"), None),
        ),
        check_vma=False,
    )
```

profile of v0, /device:TPU:0, one launch (start us, length us, event | category | flops | bytes accessed | tf_op | source)
XLA Modules:
  0.0 1007.8 jit_solution(13707422682799377687)
XLA Ops:
  7.2 5.1 multiply_reduce_fusion.1
  14.5 10.5 %all_to_all.16 = s32[8,1,4]{2,1,0:T(1,128)S(1)} all-to-all(s32[8,1,4]{2,1,0:T(1,128)S(1)} %copy.33), channel_id=1, replica_groups=mesh['group'=8,'member'=16] {'group'}, dimensions={0} | all-to-all | bytes 256 | tf_op jit(solution)/shard_map/all_to_all | solution.py:59
  25.3 42.7 %all-gather.2.cloned.1.call-done = bf16[2048,1024]{1,0:T(8,128)(2,1)} async-done(((bf16[128,1024]{1,0:T(8,128)(2,1)}), bf16[2048,1024]{1,0:T(8,128)(2,1)}) %all-gather.2.cloned.1.call-update) | async-done | bytes 4194320 | tf_op jit(solution)/shard_map/all_gather | solution.py:37
  68.0 5.0 gather_fusion
  73.0 4.5 broadcast_multiply_fusion
  77.4 4.6 all-to-all-start.1
  82.3 4.9 multiply_reduce_fusion.2
  89.6 42.0 %all-to-all-done.1 = bf16[8,4,64,1024]{3,2,1,0:T(8,128)(2,1)} async-done(((bf16[8,4,64,1024]{3,2,1,0:T(8,128)(2,1)}), bf16[8,4,64,1024]{3,2,1,0:T(8,128)(2,1)}, u32[]{:S(2)}, u32[]{:S(2)}) %all-to-all-start.1) | async-done | bytes 4194336 | tf_op jit(solution)/shard_map/all_to_all | solution.py:74
  131.6 3.8 fusion.14
  135.9 3.4 convolution_convert_fusion.2
  139.2 4.5 all-to-all-start.2
  145.3 48.2 %all-to-all-done.2 = bf16[8,4,64,1024]{3,2,1,0:T(8,128)(2,1)} async-done(((bf16[8,4,64,1024]{3,2,1,0:T(8,128)(2,1)}), bf16[8,4,64,1024]{3,2,1,0:T(8,128)(2,1)}, u32[]{:S(2)}, u32[]{:S(2)}) %all-to-all-start.2) | async-done | bytes 4194336 | tf_op jit(solution)/shard_map/all_to_all | solution.py:95
  193.5 4.5 copy.41
  198.0 4.6 fusion.4
  202.5 7.5 reshape.206
  210.0 6.8 add_convert_fusion
  217.1 3.1 fusion.12
  223.6 8.1 fusion.15
  231.7 60.6 %reduce-scatter.5.cloned.1.call-done = bf16[128,1024]{1,0:T(8,128)(2,1)} async-done(((bf16[2048,1024]{1,0:T(8,128)(2,1)}), bf16[128,1024]{1,0:T(8,128)(2,1)}) %reduce-scatter.5.cloned.1.call-update) | async-done | bytes 262160 | tf_op jit(solution)/shard_map/reduce_scatter | solution.py:121
  294.6 13.9 %add_bitcast_fusion = f32[4096,1024]{0,1:T(8,128)} fusion(f32[1024,4096]{1,0:T(8,128)} %fusion.15, bf16[128,1024]{1,0:T(8,128)(2,1)S(1)} %fusion.3, bf16[128,4096]{1,0:T(8,128)(2,1)S(1)} %copy-done.7), kind=kOutput, calls=%fused_computation.1 | convolution fusion | flops 1077936128 | bytes 34865152 | tf_op jit(solution)/shard_map/qd,qe->de/dot_general | solution.py:134
  308.4 17.5 %copy.39 = f32[4096,1024]{1,0:T(8,128)} copy(f32[4096,1024]{0,1:T(8,128)} %add_bitcast_fusion) | data formatting | bytes 33554432
  325.9 7.3 convolution_convert_fusion.1
  333.2 7.3 convolution_convert_fusion
  340.6 660.7 %reduce-scatter.7.cloned.1.call-done = f32[32,1024]{1,0:T(8,128)} async-done(((f32[4096,1024]{1,0:T(8,128)}), f32[32,1024]{1,0:T(8,128)}) %reduce-scatter.7.cloned.1.call-update) | async-done | bytes 131088
  (61 shorter events, 13.0 us)
Async XLA Ops:
  7.2 75.1 %copy-start = (bf16[128,4096]{1,0:T(8,128)(2,1)S(1)}, bf16[128,4096]{1,0:T(8,128)(2,1)}, u32[]{:S(2)}) copy-start(bf16[128,4096]{1,0:T(8,128)(2,1)} %param.5) | copy-start | bytes 3145732
  7.2 6.8 copy-start.9
  7.2 60.8 %all-gather.2.cloned.1.call-start = ((), (), s32[]{:S(2)}) async-start(), calls=%async_computation.5 | async-start | bytes 4456448 | tf_op jit(solution)/shard_map/all_gather | solution.py:37
  12.4 0.8 copy-start.3
  77.4 54.2 %all-to-all-start.1 = ((bf16[8,4,64,1024]{3,2,1,0:T(8,128)(2,1)}), bf16[8,4,64,1024]{3,2,1,0:T(8,128)(2,1)}, u32[]{:S(2)}, u32[]{:S(2)}) async-start(bf16[8,4,64,1024]{3,2,1,0:T(8,128)(2,1)} %broadcast_multiply_fusion), calls=%async_computation.1 | async-start | bytes 8388608 | tf_op jit(solution)/shard_map/all_to_all | solution.py:74
  82.3 4.9 copy-start.8
  82.3 5.8 copy-start.2
  87.1 0.8 copy-start.5
  139.2 54.2 %all-to-all-start.2 = ((bf16[8,4,64,1024]{3,2,1,0:T(8,128)(2,1)}), bf16[8,4,64,1024]{3,2,1,0:T(8,128)(2,1)}, u32[]{:S(2)}, u32[]{:S(2)}) async-start(bf16[8,4,64,1024]{3,2,1,0:T(8,128)(2,1)} %bitcast.58), calls=%async_computation.2 | async-start | bytes 8388608 | tf_op jit(solution)/shard_map/all_to_all | solution.py:95
  143.8 148.5 %reduce-scatter.5.cloned.1.call-start = ((), (), s32[]{:S(2)}) async-start(), calls=%async_computation.6 | async-start | bytes 4456448 | tf_op jit(solution)/shard_map/reduce_scatter | solution.py:121
  216.9 784.4 %reduce-scatter.7.cloned.1.call-start = ((), (), s32[]{:S(2)}) async-start(), calls=%async_computation.7 | async-start | bytes 16908288
  217.1 3.1 copy-start.6
  223.5 68.7 %copy-start.4 = (f32[128,1024]{1,0:T(8,128)S(1)}, f32[128,1024]{1,0:T(8,128)}, u32[]{:S(2)}) copy-start(f32[128,1024]{1,0:T(8,128)} %copy-done.3) | copy-start | bytes 1572868
  223.6 71.0 %copy-start.7 = (bf16[128,4096]{1,0:T(8,128)(2,1)S(1)}, bf16[128,4096]{1,0:T(8,128)(2,1)}, u32[]{:S(2)}) copy-start(bf16[128,4096]{1,0:T(8,128)(2,1)} %param.6) | copy-start | bytes 3145732
  325.9 675.4 %copy-start.1 = (bf16[128,4096]{1,0:T(8,128)(2,1)S(1)}, bf16[128,4096]{1,0:T(8,128)(2,1)}, u32[]{:S(2)}) copy-start(bf16[128,4096]{1,0:T(8,128)(2,1)} %param.5) | copy-start | bytes 3145732
Sparse Core Ops, SparseCore 0:
  14.1 53.8 all-gather.1
  217.0 75.2 reduce-scatter.4
  326.0 675.1 reduce-scatter.6
where the time goes:
time: 1010 us
  waiting for transfers between devices  854 us (85%)
  matrix products  72.9 us (7%)
  local copies, waits for them, and re-layouts  37.3 us (4%)
  between operations  14 us (1%)
  blocking collectives  10.5 us (1%)
    unnamed x4, waiting for transfers between devices  661 us
    reduce_scatter x1, waiting for transfers between devices, body(): lax.psum_scatter(code_terms.astype(jnp.bfloat16), 'member', scatter_dimen...  60.6 us
    all_to_all x1, waiting for transfers between devices, body(): lax.all_to_all(outgoing.reshape(groups, capacity, CB, emb_width), 'group'...  48.2 us
    all_gather x1, waiting for transfers between devices, body(): group_codes = lax.all_gather(c_emb, 'member', axis=0, tiled=True)  42.7 us
    all_to_all x1, waiting for transfers between devices, body(): lax.all_to_all(picked, 'group', split_axis=0, concat_axis=0, tiled=True)  42 us
    unnamed x22, local copies, waits for them, and re-layouts  23.6 us
  transfers between devices with their start and end apart: 5, of which 5 were waited for; matrix products, arithmetic and copies ran while one was open for 4% of the time, Pallas kernels for 0%

commit v1 on v0

v1 whole, which is shorter than its diff:
```python
import functools

import jax
import jax.numpy as jnp
from jax import lax
from jax.experimental import pallas as pl
from jax.experimental.pallas import tpu as pltpu
from jax.sharding import PartitionSpec as P

MESH = pl.DeviceIdType.MESH
F32 = jnp.float32
BF16 = jnp.bfloat16
inverse_temp = 120.0
epsilon = 1e-06
LOW = -1e30

PLACE = {2: 0, 1: 1, 3: 2, 0: 3}
LINE = [(dz, dk) for dz in (2, 1, 3, 0) for dk in (0, 1)]
PEERS = [p for p in LINE if p != (0, 0)]


def slot(dz, dk):
    return 2 * PLACE[dz % 4] + dk % 2


OWN = slot(0, 0)


class Links:
    def __init__(self, send, recv):
        self.send, self.recv, self.made = send, recv, []
        group, member = lax.axis_index("group"), lax.axis_index("member")
        self.z, self.core = group // 2, group % 2
        self.x, self.y = member // 4, member % 4

    def device(self, dx=0, dy=0, dz=0, dk=0):
        group = 2 * ((self.z + dz % 4) % 4) + (self.core + dk) % 2
        member = 4 * ((self.x + dx % 4) % 4) + (self.y + dy % 4) % 4
        return (group, member)

    def start(self, src, dst, **where):
        i = len(self.made)
        copy = pltpu.make_async_remote_copy(
            src_ref=src,
            dst_ref=dst,
            send_sem=self.send.at[i],
            recv_sem=self.recv.at[i],
            device_id=self.device(**where),
            device_id_type=MESH,
        )
        copy.start()
        self.made.append(copy)
        return copy

    def barrier(self, places):
        sem = pltpu.get_barrier_semaphore()
        for where in places:
            pl.semaphore_signal(sem, inc=1, device_id=self.device(**where), device_id_type=MESH)
        pl.semaphore_wait(sem, len(places))

    def drain(self):
        for copy in self.made:
            copy.wait_send()


def dot_nt(a, b):
    return lax.dot_general(a, b, (((1,), (1,)), ((), ())), preferred_element_type=F32)


def dot_tn(a, b):
    return lax.dot_general(a, b, (((0,), (0,)), ((), ())), preferred_element_type=F32)


def add_into(dst, *terms):
    total = terms[0].astype(F32)
    for term in terms[1:]:
        total = total + term.astype(F32)
    dst[...] = total.astype(dst.dtype)


def norm_back(upstream, unit, inverse):
    inner = jnp.sum(unit * upstream, axis=1, keepdims=True)
    return (inverse * (upstream - unit * inner)).astype(BF16)


def attend(
    q_ref, c_ref, note_ref, qu_ref, qi_ref, cu_ref, ci_ref, qf_ref, cf_ref,
    dz_ref, half_ref,
    queries, codes, scores, grads, dcode, dquery, notes, mine, stats, top, mass, lse, scale,
    yp0, ym0, yp1, ym1, xp0, xm0, xp1, xm1, sib, zp0, zm0, zp1, zm1, low_a, low_b, dc_sum,
    send, recv, local,
):
    width = q_ref.shape[1]
    link = Links(send, recv)
    link.barrier(
        [dict(dx=1), dict(dx=-1), dict(dy=1), dict(dy=-1)]
        + [dict(dz=dz, dk=dk) for dz, dk in PEERS]
    )

    def q_rows(dz, dk, at=0, n=128):
        return queries.at[pl.ds(128 * slot(dz, dk) + at, n)]

    def code(half, first, second, at=0, n=64):
        return codes.at[pl.ds(256 * (4 * half + second) + 64 * first + at, n)]

    axes = (("dx", "dy"), ("dy", "dx"))

    note_in = {}
    for dz, dk in PEERS:
        s, r = slot(dz, dk), slot(-dz, dk)
        note_in[r] = link.start(note_ref.at[s], notes.at[r], dz=dz, dk=dk)
    codes[0:64] = c_ref[0:64]
    codes[1024:1088] = c_ref[64:128]
    queries[pl.ds(128 * OWN, 128)] = q_ref[...]
    notes[OWN] = note_ref[OWN]
    near = {}
    for h in (0, 1):
        a = axes[h][0]
        near[h, 3] = link.start(code(h, 0, 0), code(h, 3, 0), **{a: 1})
        near[h, 1] = link.start(code(h, 0, 0), code(h, 1, 0), **{a: -1})
    q_in = {}
    q_in[3] = link.start(q_ref, q_rows(3, 0), dz=1)
    q_in[1] = link.start(q_ref, q_rows(1, 0), dz=-1)
    s_in = {0: link.start(q_ref, q_rows(0, 1), dk=1)}

    step = {}

    def spread(h, f):
        b = axes[h][1]
        step[h, f, 3] = link.start(code(h, f, 0), code(h, f, 3), **{b: 1})
        step[h, f, 1] = link.start(code(h, f, 0), code(h, f, 1), **{b: -1})

    far = {}
    for h in (0, 1):
        spread(h, 0)
    for h in (0, 1):
        a = axes[h][0]
        near[h, 1].wait_recv()
        far[h, 0] = link.start(code(h, 1, 0, 0, 32), code(h, 2, 0, 0, 32), **{a: -1})
        spread(h, 1)
        near[h, 3].wait_recv()
        far[h, 1] = link.start(code(h, 3, 0, 32, 32), code(h, 2, 0, 32, 32), **{a: 1})
        spread(h, 3)

    moves, shared = [], []
    for i, f_ref in enumerate((qf_ref, cf_ref)):
        for zz in range(4):
            keep = pl.ds(pl.multiple_of((2 * zz + link.core) * 512, 512), 512)
            give = pl.ds(pl.multiple_of((2 * zz + 1 - link.core) * 512, 512), 512)
            move = pltpu.make_async_copy(
                f_ref.at[:, keep],
                half_ref.at[pl.ds(128 * i, 128), pl.ds(512 * zz, 512)],
                local.at[4 * i + zz],
            )
            move.start()
            moves.append(move)
            shared.append(
                link.start(
                    f_ref.at[:, give],
                    half_ref.at[pl.ds(256 + 128 * i, 128), pl.ds(512 * zz, 512)],
                    dk=1,
                )
            )

    top[...] = jnp.full(top.shape, LOW, F32)
    mass[...] = jnp.zeros(mass.shape, F32)

    q_in[1].wait_recv()
    q_far0 = link.start(q_rows(1, 0, 0, 64), q_rows(2, 0, 0, 64), dz=-1)
    s_in[1] = link.start(q_rows(1, 0), q_rows(1, 1), dk=1)
    q_in[3].wait_recv()
    q_far1 = link.start(q_rows(3, 0, 64, 64), q_rows(2, 0, 64, 64), dz=1)
    s_in[3] = link.start(q_rows(3, 0), q_rows(3, 1), dk=1)
    for h in (0, 1):
        far[h, 0].wait_recv()
        far[h, 1].wait_recv()
        spread(h, 2)

    last = {}

    def onward(f):
        for h in (0, 1):
            b = axes[h][1]
            step[h, f, 1].wait_recv()
            last[h, f, 0] = link.start(code(h, f, 1, 0, 32), code(h, f, 2, 0, 32), **{b: -1})
            step[h, f, 3].wait_recv()
            last[h, f, 1] = link.start(code(h, f, 3, 32, 32), code(h, f, 2, 32, 32), **{b: 1})

    def score(t):
        rows = pl.ds(256 * t, 256)

        def part(j, carry):
            lanes = pl.ds(pl.multiple_of(256 * j, 256), 256)
            s = inverse_temp * dot_nt(codes[rows], queries[pl.ds(pl.multiple_of(256 * j, 256), 256)])
            pieces = []
            for u in range(4):
                bias = jnp.concatenate(
                    [notes[2 * j, 4 * t + u : 4 * t + u + 1], notes[2 * j + 1, 4 * t + u : 4 * t + u + 1]],
                    axis=1,
                )
                pieces.append(s[64 * u : 64 * u + 64] + bias)
            s = jnp.concatenate(pieces, axis=0)
            scores[rows, lanes] = s
            before = top[:, lanes]
            after = jnp.maximum(before, jnp.max(s, axis=0, keepdims=True))
            mass[:, lanes] = mass[:, lanes] * jnp.exp(before - after) + jnp.sum(
                jnp.exp(s - after), axis=0, keepdims=True
            )
            top[:, lanes] = after
            return carry

        lax.fori_loop(0, 4, part, 0)

    onward(0)
    onward(1)
    q_far0.wait_recv()
    q_far1.wait_recv()
    s_in[2] = link.start(q_rows(2, 0), q_rows(2, 1), dk=1)
    onward(3)
    for copy in note_in.values():
        copy.wait_recv()
    for dz in (0, 1, 3, 2):
        s_in[dz].wait_recv()
    score(0)
    score(4)
    onward(2)
    for t in (1, 3, 5, 7):
        score(t)
    for h in (0, 1):
        for f in range(4):
            last[h, f, 0].wait_recv()
            last[h, f, 1].wait_recv()
        score(4 * h + 2)

    for s in range(8):
        mine[s : s + 1] = top[:, 128 * s : 128 * s + 128]
        mine[8 + s : 9 + s] = mass[:, 128 * s : 128 * s + 128]
    told = []
    for dz, dk in PEERS:
        told.append(link.start(mine, stats.at[slot(-dz, dk)], dz=dz, dk=dk))
    stats[OWN] = mine[...]
    for copy in told:
        copy.wait_recv()
    for tz, tk in LINE:
        t = slot(tz, tk)
        seen = [(slot(rz, rk), slot(tz - rz, tk + rk)) for rz, rk in LINE]
        most = functools.reduce(jnp.maximum, [stats[r, i : i + 1] for r, i in seen])
        whole = sum(stats[r, 8 + i : 9 + i] * jnp.exp(stats[r, i : i + 1] - most) for r, i in seen)
        lse[:, 128 * t : 128 * t + 128] = most + jnp.log(whole)
        scale[:, 128 * t : 128 * t + 128] = inverse_temp * notes[t, 32:33]

    def backward(t):
        rows = pl.ds(256 * t, 256)

        def part(j, carry):
            lanes = pl.ds(pl.multiple_of(256 * j, 256), 256)
            grads[rows, lanes] = (
                scale[:, lanes] * jnp.exp(scores[rows, lanes] - lse[:, lanes])
            ).astype(BF16)
            return carry

        lax.fori_loop(0, 4, part, 0)
        if t % 4 == 0:
            lanes = slice(128 * OWN, 128 * OWN + 128)
            own = slice(256 * t, 256 * t + 64)
            i = lax.broadcasted_iota(jnp.int32, (64, 128), 0) + 16 * t
            j = lax.broadcasted_iota(jnp.int32, (64, 128), 1)
            hit = jnp.where(i == j, 1.0, 0.0).astype(F32)
            grads[own, lanes] = (
                scale[:, lanes] * (jnp.exp(scores[own, lanes] - lse[:, lanes]) - hit)
            ).astype(BF16)

        def product(n, carry):
            cols = pl.ds(pl.multiple_of(256 * n, 256), 256)
            dcode[rows, cols] = jnp.dot(
                grads[rows, :], queries[:, cols], preferred_element_type=F32
            ).astype(BF16)
            return carry

        lax.fori_loop(0, width // 256, product, 0)

    def tile(h, t, at, n):
        return dcode.at[pl.ds(256 * (4 * h + t) + at, n)]

    back = {}
    for h in (0, 1):
        b = axes[h][1]
        backward(4 * h + 2)
        back[h, "p0"] = link.start(tile(h, 2, 0, 128), yp0.at[h], **{b: 1})
        back[h, "m0"] = link.start(tile(h, 2, 128, 128), ym0.at[h], **{b: -1})
    for h in (0, 1):
        b = axes[h][1]
        backward(4 * h + 1)
        back[h, "p1"] = link.start(tile(h, 1, 128, 128), yp1.at[h, pl.ds(128, 128)], **{b: 1})
        backward(4 * h + 3)
        back[h, "m1"] = link.start(tile(h, 3, 0, 128), ym1.at[h, pl.ds(0, 128)], **{b: -1})
    for h in (0, 1):
        b = axes[h][1]
        back[h, "p0"].wait_recv()
        add_into(tile(h, 1, 0, 128), tile(h, 1, 0, 128)[...], yp0[h])
        back[h, "p2"] = link.start(tile(h, 1, 0, 128), yp1.at[h, pl.ds(0, 128)], **{b: 1})
        back[h, "m0"].wait_recv()
        add_into(tile(h, 3, 128, 128), tile(h, 3, 128, 128)[...], ym0[h])
        back[h, "m2"] = link.start(tile(h, 3, 128, 128), ym1.at[h, pl.ds(128, 128)], **{b: -1})
    backward(0)
    backward(4)

    home = {}
    for p, dz in enumerate((2, 1, 3, 0)):
        at = pl.ds(256 * p, 256)
        lhs = grads[:, 256 * p : 256 * p + 256]

        def product(n, carry, lhs=lhs, at=at):
            cols = pl.ds(pl.multiple_of(256 * n, 256), 256)
            dquery[at, cols] = dot_tn(lhs, codes[:, cols]).astype(BF16)
            return carry

        lax.fori_loop(0, width // 256, product, 0)
        home[dz] = link.start(dquery.at[pl.ds(256 * p + 128, 128)], sib.at[p], dk=1)

    def dq(dz, at=0, n=128):
        return dquery.at[pl.ds(128 * slot(dz, 0) + at, n)]

    for dz in (2, 1, 3):
        home[dz].wait_recv()
        add_into(dq(dz), dq(dz)[...], sib[PLACE[dz]])
        if dz == 2:
            z0p = link.start(dq(2, 0, 64), zp0, dz=1)
            z0m = link.start(dq(2, 64, 64), zm0, dz=-1)
        elif dz == 1:
            z1p = link.start(dq(1, 64, 64), zp1.at[pl.ds(64, 64)], dz=1)
        else:
            z1m = link.start(dq(3, 0, 64), zm1.at[pl.ds(0, 64)], dz=-1)

    def inner(h):
        a = axes[h][0]
        for name in ("p1", "p2", "m1", "m2"):
            back[h, name].wait_recv()
        low = (low_a, low_b)[h]
        for f in (2, 1, 3, 0):
            s = slice(64 * f, 64 * f + 64)
            total = (
                tile(h, 0, 64 * f, 64)[...].astype(F32)
                + yp1[h, s].astype(F32)
                + ym1[h, s].astype(F32)
            )
            if f == 0:
                dc_sum[64 * h : 64 * h + 64] = total
            else:
                low[s] = total.astype(BF16)
            if f == 2:
                back[h, "q0"] = link.start(low.at[pl.ds(128, 32)], xp0.at[h], **{a: 1})
                back[h, "n0"] = link.start(low.at[pl.ds(160, 32)], xm0.at[h], **{a: -1})
            if f == 1:
                back[h, "q1"] = link.start(low.at[pl.ds(96, 32)], xp1.at[h, pl.ds(32, 32)], **{a: 1})
            if f == 3:
                back[h, "n1"] = link.start(low.at[pl.ds(192, 32)], xm1.at[h, pl.ds(0, 32)], **{a: -1})

    def outer(h):
        a = axes[h][0]
        low = (low_a, low_b)[h]
        back[h, "q0"].wait_recv()
        add_into(low.at[pl.ds(64, 32)], low[64:96], xp0[h])
        back[h, "q2"] = link.start(low.at[pl.ds(64, 32)], xp1.at[h, pl.ds(0, 32)], **{a: 1})
        back[h, "n0"].wait_recv()
        add_into(low.at[pl.ds(224, 32)], low[224:256], xm0[h])
        back[h, "n2"] = link.start(low.at[pl.ds(224, 32)], xm1.at[h, pl.ds(32, 32)], **{a: -1})

    z0p.wait_recv()
    add_into(dq(1, 0, 64), dq(1, 0, 64)[...], zp0[...])
    z2p = link.start(dq(1, 0, 64), zp1.at[pl.ds(0, 64)], dz=1)
    z0m.wait_recv()
    add_into(dq(3, 64, 64), dq(3, 64, 64)[...], zm0[...])
    z2m = link.start(dq(3, 64, 64), zm1.at[pl.ds(64, 64)], dz=-1)
    inner(0)
    inner(1)
    home[0].wait_recv()
    for copy in (z1p, z2p, z1m, z2m):
        copy.wait_recv()
    d_q = (
        dq(0)[...].astype(F32)
        + sib[PLACE[0]].astype(F32)
        + zp1[...].astype(F32)
        + zm1[...].astype(F32)
    )
    dz_ref[0:128] = norm_back(d_q, qu_ref[...], qi_ref[...])
    pair_q = link.start(dz_ref.at[pl.ds(0, 128)], dz_ref.at[pl.ds(256, 128)], dk=1)
    outer(0)
    outer(1)
    for h in (0, 1):
        for name in ("q1", "q2", "n1", "n2"):
            back[h, name].wait_recv()
        s = slice(64 * h, 64 * h + 64)
        dc_sum[s] = dc_sum[s] + xp1[h].astype(F32) + xm1[h].astype(F32)
    dz_ref[128:256] = norm_back(dc_sum[...], cu_ref[...], ci_ref[...])
    pair_c = link.start(dz_ref.at[pl.ds(128, 128)], dz_ref.at[pl.ds(384, 128)], dk=1)
    pair_q.wait_recv()
    pair_c.wait_recv()
    for move in moves:
        move.wait()
    for copy in shared:
        copy.wait_recv()
    link.drain()


N_ATTEND = 7 + 4 + 3 + 16 + 4 + 8 + 2 + 3 + 16 + 7 + 12 + 4 + 6 + 12 + 2


PARTS = ((0, 384, "zxy"), (384, 384, "xyz"), (768, 256, "yzx"))


def finish(dz_ref, half_ref, w_hbm, qg_ref, cg_ref, pg_ref, weights, partial, *rest):
    boxes, (send, recv, local) = rest[:-3], rest[-3:]
    link = Links(send, recv)
    fetch = pltpu.make_async_copy(w_hbm, weights, local)
    fetch.start()
    link.barrier([{f"d{a}": s} for a in "xyz" for s in (1, -1)])
    here = {"x": link.x, "y": link.y, "z": link.z}
    per = len(boxes) // len(PARTS)
    rows_q = pg_ref.shape[0]
    low, high = pl.ds(0, rows_q // 2), pl.ds(rows_q // 2, rows_q // 2)

    class Part:
        def __init__(self, i):
            self.at, self.n, self.order = PARTS[i]
            self.boxes = boxes[per * i : per * i + per]
            self.left = "zxy"
            self.level = 0
            self.value = None

        def chunk(self, d, rows=slice(None)):
            axis = self.order[self.level]
            index = tuple(
                (here[a] + d) % 4 if a == axis else slice(None) for a in self.left
            )
            if self.level == 0:
                return partial.at[index + (rows, pl.ds(self.at, self.n))]
            return self.value.at[index + (rows,)]

        def box(self, name):
            return self.boxes[5 * self.level + ("p0", "m0", "p1", "m1", "sum").index(name)]

        def rows_of(self, ref, rows):
            return ref.at[(slice(None),) * (len(self.left) - 1) + (rows,)]

        def open(self):
            name = "d" + self.order[self.level]
            self.c = {}
            self.c["p0"] = link.start(self.chunk(2, low), self.box("p0"), **{name: 1})
            self.c["m0"] = link.start(self.chunk(2, high), self.box("m0"), **{name: -1})
            self.c["p1"] = link.start(
                self.chunk(1, high), self.rows_of(self.box("p1"), high), **{name: 1}
            )
            self.c["m1"] = link.start(
                self.chunk(3, low), self.rows_of(self.box("m1"), low), **{name: -1}
            )

        def merge(self, dst, *terms):
            if len(dst.shape) <= 2:
                add_into(dst, *[t[...] for t in terms])
                return

            def body(i, carry):
                add_into(dst.at[i], *[t[i] for t in terms])
                return carry

            lax.fori_loop(0, dst.shape[0], body, 0)

        def relay(self):
            name = "d" + self.order[self.level]
            self.c["p0"].wait_recv()
            self.merge(self.chunk(1, low), self.chunk(1, low), self.box("p0"))
            self.c["p2"] = link.start(
                self.chunk(1, low), self.rows_of(self.box("p1"), low), **{name: 1}
            )
            self.c["m0"].wait_recv()
            self.merge(self.chunk(3, high), self.chunk(3, high), self.box("m0"))
            self.c["m2"] = link.start(
                self.chunk(3, high), self.rows_of(self.box("m1"), high), **{name: -1}
            )

        def close(self):
            for key in ("p1", "p2", "m1", "m2"):
                self.c[key].wait_recv()
            terms = (self.chunk(0), self.box("p1"), self.box("m1"))
            if self.level == 2:
                total = sum(t[...].astype(F32) for t in terms)
                pg_ref[:, self.at : self.at + self.n] = total
                return
            done = self.box("sum")
            self.merge(done, *terms)
            self.value = done
            self.left = self.left.replace(self.order[self.level], "")
            self.level += 1

    parts = [Part(i) for i in range(len(PARTS))]
    for part in (parts[2], parts[0], parts[1]):
        cols = pl.ds(part.at, part.n)

        def product(i, carry, cols=cols, n=part.n):
            rows = pl.ds(pl.multiple_of(256 * i, 256), 256)
            value = dot_tn(half_ref[:, rows], dz_ref[:, cols]).astype(BF16)
            partial[i // 2, pl.ds(2 * (i % 2), 2), :, :, cols] = value.reshape(2, 4, 32, n)
            return carry

        lax.fori_loop(0, 8, product, 0)
        part.open()

    fetch.wait()

    def features(i, carry):
        rows = pl.ds(pl.multiple_of(256 * i, 256), 256)
        value = dot_nt(dz_ref[0:256], weights[rows]).astype(BF16)
        qg_ref[:, rows] = value[0:128]
        cg_ref[:, rows] = value[128:256]
        return carry

    order = (parts[2], parts[0], parts[1])
    lax.fori_loop(0, 8, features, 0)
    for part in order:
        part.relay()
    lax.fori_loop(8, 16, features, 0)
    for part in order:
        part.close()
        part.open()
    for level in (1, 2):
        for part in order:
            part.relay()
        for part in order:
            part.close()
            if level == 1:
                part.open()
    link.drain()


def embed(features, projection):
    values = jnp.dot(features, projection, preferred_element_type=F32)
    inverse = lax.rsqrt(jnp.sum(values * values, axis=1, keepdims=True) + epsilon)
    unit_vec = values * inverse
    return (unit_vec, inverse, unit_vec.astype(BF16))


def notes_of(hard_ids, loss_weight):
    group, member = lax.axis_index("group"), lax.axis_index("member")
    z, core, x, y = group // 2, group % 2, member // 4, member % 4
    line = jnp.array(LINE, jnp.int32)
    at = 2 * ((z + line[:, 0]) % 4) + (core + line[:, 1]) % 2
    t = jnp.arange(8, dtype=jnp.int32)[:, None]
    u = jnp.arange(4, dtype=jnp.int32)[None, :]
    dx = jnp.where(t < 4, u, t - 4)
    dy = jnp.where(t < 4, t, u)
    block = ((4 * ((x + dx) % 4) + (y + dy) % 4) * 2 + t // 4).reshape(-1)
    ids = at[:, None] * 32 + block[None, :]
    wanted = jnp.any(ids[:, :, None] == hard_ids[0][None, None, :], axis=2)
    wanted = wanted | (at == group)[:, None]
    bias = jnp.where(wanted, 0.0, LOW).astype(F32)
    bias = jnp.broadcast_to(bias[:, :, None], (8, 32, 128))
    weight = jnp.broadcast_to(loss_weight[None, None, :], (8, 8, 128))
    return jnp.concatenate([bias, weight], axis=1)


def body(query_feat, code_feat, projection, hard_ids, loss_weight):
    rows, depth = query_feat.shape
    width = projection.shape[1]
    q_unit, q_inv, q_emb = embed(query_feat, projection)
    c_unit, c_inv, c_emb = embed(code_feat, projection)
    notes = notes_of(hard_ids, loss_weight)
    vmem = pl.BlockSpec(memory_space=pltpu.VMEM)
    anywhere = pl.BlockSpec(memory_space=pl.ANY)

    def vm(*shape, dtype=BF16):
        return pltpu.VMEM(shape, dtype)

    dz, half = pl.pallas_call(
        attend,
        out_shape=(
            jax.ShapeDtypeStruct((4 * rows, width), BF16),
            jax.ShapeDtypeStruct((4 * rows, depth // 2), BF16),
        ),
        in_specs=[vmem] * 7 + [anywhere] * 2,
        out_specs=(vmem, anywhere),
        scratch_shapes=[
            vm(1024, width),
            vm(2048, width),
            vm(2048, 1024, dtype=F32),
            vm(2048, 1024),
            vm(2048, width),
            vm(1024, width),
            vm(8, 40, 128, dtype=F32),
            vm(16, 128, dtype=F32),
            vm(8, 16, 128, dtype=F32),
            vm(1, 1024, dtype=F32),
            vm(1, 1024, dtype=F32),
            vm(1, 1024, dtype=F32),
            vm(1, 1024, dtype=F32),
            vm(2, 128, width),
            vm(2, 128, width),
            vm(2, 256, width),
            vm(2, 256, width),
            vm(2, 32, width),
            vm(2, 32, width),
            vm(2, 64, width),
            vm(2, 64, width),
            vm(4, 128, width),
            vm(64, width),
            vm(64, width),
            vm(128, width),
            vm(128, width),
            vm(256, width),
            vm(256, width),
            vm(128, width, dtype=F32),
            pltpu.SemaphoreType.DMA((N_ATTEND,)),
            pltpu.SemaphoreType.DMA((N_ATTEND,)),
            pltpu.SemaphoreType.DMA((8,)),
        ],
        compiler_params=pltpu.CompilerParams(
            collective_id=0, has_side_effects=True, vmem_limit_bytes=56 * 2**20
        ),
        name="attend",
    )(q_emb, c_emb, notes, q_unit, q_inv, c_unit, c_inv, query_feat, code_feat)

    boxes = []
    for _, n, _ in PARTS:
        for dims in ((4, 4), (4,), ()):
            boxes += [vm(*dims, 16, n)] * 2 + [vm(*dims, 32, n)] * 3
    return tuple(
        pl.pallas_call(
            finish,
            out_shape=(
                jax.ShapeDtypeStruct((rows, depth), BF16),
                jax.ShapeDtypeStruct((rows, depth), BF16),
                jax.ShapeDtypeStruct((depth // 128, width), F32),
            ),
            in_specs=[vmem, vmem, anywhere],
            out_specs=(vmem, vmem, vmem),
            scratch_shapes=[vm(depth, width), vm(4, 4, 4, 32, width), *boxes]
            + [
                pltpu.SemaphoreType.DMA((54,)),
                pltpu.SemaphoreType.DMA((54,)),
                pltpu.SemaphoreType.DMA,
            ],
            compiler_params=pltpu.CompilerParams(
                collective_id=1, has_side_effects=True, vmem_limit_bytes=56 * 2**20
            ),
            name="finish",
        )(dz, half, projection)
    )


def solution(mesh):
    lined = P(("group", "member"), None)
    return jax.shard_map(
        body,
        mesh=mesh,
        in_specs=(lined, lined, P(), lined, P(("group", "member"))),
        out_specs=(lined, lined, lined),
        check_vma=False,
    )
```

time: 1010 us -> 150 us (0.15)
  the two profiles are of different devices: /device:TPU:0 before, /device:TPU:1 now
where the time goes in v1:
time: 150 us; the launch traced here: 148 us
  Pallas kernels  125 us (83%)
  matrix products  9.77 us (7%)
  local copies, waits for them, and re-layouts  8.7 us (6%)
  other arithmetic  3.65 us (2%)
    pallas_call x1, Pallas kernels, body(): pl.pallas_call(attend, out_shape=(jax.ShapeDtypeStruct((4 * rows, width),...  87 us
    pallas_call x1, Pallas kernels, body(): pl.pallas_call(finish, out_shape=(jax.ShapeDtypeStruct((rows, depth), BF1...  38.2 us
    dot_general x2, matrix products, embed(): values = jnp.dot(features, projection, preferred_element_type=F32)  9.77 us
    unnamed x5, local copies, waits for them, and re-layouts  6.15 us

profile of v1, /device:TPU:1, one launch (start us, length us, event | category | flops | bytes accessed | tf_op | source)
XLA Modules:
  0.0 148.0 jit_solution(4666836986587081362)
XLA Ops:
  0.7 0.7 compare_bitcast_fusion
  1.4 0.1 add.185
  1.5 0.1 add.186
  1.6 0.1 select_add_fusion.1
  1.6 0.1 add.177
  1.7 0.1 add.182
  1.8 0.1 broadcast_add_fusion
  1.9 0.8 compare_reduce_fusion
  2.6 0.1 or_select_fusion
  2.7 0.7 broadcast_in_dim.83
  3.4 0.1 broadcast_in_dim.82
  3.5 0.0 copy-start
  3.5 0.7 pad_maximum_fusion.note_ref
  4.2 5.1 %multiply_reduce_fusion.1 = (f32[128]{0:T(128)S(1)}, f32[128,1024]{1,0:T(8,128)S(1)}) fusion(bf16[128,4096]{1,0:T(8,128)(2,1)} %qf_ref.1, bf16[4096,1024]{1,0:T(8,128)(2,1)} %w_hbm.1), kind=kOutput, calls=%fused_computation.1 | convolution fusion | flops 1074003840 | bytes 9961984 | tf_op jit(solution)/shard_map/dot_general | solution.py:537
  9.2 0.8 copy.13.qi_ref
  10.0 0.0 copy-done
  10.0 4.7 %multiply_reduce_fusion = (f32[128]{0:T(128)S(1)}, f32[128,1024]{1,0:T(8,128)S(1)}) fusion(bf16[128,4096]{1,0:T(8,128)(2,1)S(1)} %copy-done, bf16[4096,1024]{1,0:T(8,128)(2,1)} %w_hbm.1), kind=kOutput, calls=%fused_computation | convolution fusion | flops 1074003840 | bytes 9961984 | tf_op jit(solution)/shard_map/dot_general | solution.py:537
  14.7 0.7 copy.14.ci_ref
  15.5 1.3 fusion.11
  16.7 87.0 %attend.1 = (bf16[512,1024]{1,0:T(8,128)(2,1)}, bf16[512,2048]{1,0:T(8,128)(2,1)}) custom-call(bf16[128,1024]{1,0:T(8,128)(2,1)} %get-tuple-element.23.q_ref, bf16[128,1024]{1,0:T(8,128)(2,1)} %get-tuple-element.9.c_ref, f32[8,40,128]{2,1,0:T(8,128)} %pad_maximum_fusion.note_ref, f32[128,1024]{1,0:T(8,128)} %get-tuple-element.24.qu_ref, ...), custom_call_target="tpu_custom_call" | custom-call | tf_op jit(solution)/shard_map/attend/pallas_call | solution.py:574
  103.7 38.2 %finish.1 = (bf16[128,4096]{1,0:T(8,128)(2,1)}, bf16[128,4096]{1,0:T(8,128)(2,1)}, f32[32,1024]{1,0:T(8,128)}) custom-call(bf16[512,1024]{1,0:T(8,128)(2,1)} %get-tuple-element.5.dz_ref, bf16[512,2048]{1,0:T(8,128)(2,1)} %get-tuple-element.6.half_ref, bf16[4096,1024]{1,0:T(8,128)(2,1)} %w_hbm.1), custom_call_target="tpu_custom_call" | custom-call | tf_op jit(solution)/shard_map/finish/pallas_call | solution.py:627
  141.9 2.3 %copy.18 = bf16[128,4096]{1,0:T(8,128)(2,1)} copy(bf16[128,4096]{1,0:T(8,128)(2,1)} %get-tuple-element.28) | data formatting | bytes 2097152
  144.2 2.3 %copy.19 = bf16[128,4096]{1,0:T(8,128)(2,1)} copy(bf16[128,4096]{1,0:T(8,128)(2,1)} %get-tuple-element.29) | data formatting | bytes 2097152
  146.4 1.6 %copy.20 = f32[32,1024]{1,0:T(8,128)} copy(f32[32,1024]{1,0:T(8,128)} %get-tuple-element.30) | data formatting | bytes 262144
  (7 shorter events, 0.0 us)
Async XLA Ops:
  3.5 6.5 %copy-start = (bf16[128,4096]{1,0:T(8,128)(2,1)S(1)}, bf16[128,4096]{1,0:T(8,128)(2,1)}, u32[]{:S(2)}) copy-start(bf16[128,4096]{1,0:T(8,128)(2,1)} %cf_ref.1) | copy-start | bytes 3145732

commit v2 on v1

--- a/solution.py
+++ b/solution.py
@@ -52,11 +52,15 @@
         self.made.append(copy)
         return copy
 
-    def barrier(self, places):
+    def greet(self):
         sem = pltpu.get_barrier_semaphore()
+        places = [dict(dx=1), dict(dx=-1), dict(dy=1), dict(dy=-1)]
+        places += [dict(dz=dz, dk=dk) for dz, dk in PEERS]
         for where in places:
             pl.semaphore_signal(sem, inc=1, device_id=self.device(**where), device_id_type=MESH)
-        pl.semaphore_wait(sem, len(places))
+
+    def meet(self):
+        pl.semaphore_wait(pltpu.get_barrier_semaphore(), 4 + len(PEERS))
 
     def drain(self):
         for copy in self.made:
@@ -65,10 +69,6 @@
 
 def dot_nt(a, b):
     return lax.dot_general(a, b, (((1,), (1,)), ((), ())), preferred_element_type=F32)
-
-
-def dot_tn(a, b):
-    return lax.dot_general(a, b, (((0,), (0,)), ((), ())), preferred_element_type=F32)
 
 
 def add_into(dst, *terms):
@@ -83,19 +83,69 @@
     return (inverse * (upstream - unit * inner)).astype(BF16)
 
 
-def attend(
-    q_ref, c_ref, note_ref, qu_ref, qi_ref, cu_ref, ci_ref, qf_ref, cf_ref,
-    dz_ref, half_ref,
-    queries, codes, scores, grads, dcode, dquery, notes, mine, stats, top, mass, lse, scale,
+PARTS = ((0, 384, "zxy"), (384, 384, "xyz"), (768, 256, "yzx"))
+
+N_COPIES = 7 + 4 + 3 + 16 + 4 + 4 + 2 + 3 + 16 + 7 + 12 + 4 + 6 + 12 + 2 + 54
+
+
+def step(
+    qf_hbm, cf_hbm, w_hbm, ids_ref, weight_ref,
+    qg_ref, cg_ref, pg_ref,
+    outbox, weights, partial, feats, other, turned, unit, inverse, dz_ref,
+    queries, codes, scores, grads, turn, dcode, dquery, notes, mine, stats, top, mass, lse, scale,
     yp0, ym0, yp1, ym1, xp0, xm0, xp1, xm1, sib, zp0, zm0, zp1, zm1, low_a, low_b, dc_sum,
-    send, recv, local,
+    *rest,
 ):
-    width = q_ref.shape[1]
+    boxes, (send, recv, local) = rest[:-3], rest[-3:]
+    width = weights.shape[1]
     link = Links(send, recv)
-    link.barrier(
-        [dict(dx=1), dict(dx=-1), dict(dy=1), dict(dy=-1)]
-        + [dict(dz=dz, dk=dk) for dz, dk in PEERS]
-    )
+    loads = [
+        pltpu.make_async_copy(f, feats.at[pl.ds(128 * i, 128)], local.at[i])
+        for i, f in enumerate((qf_hbm, cf_hbm))
+    ]
+    fetch = [
+        pltpu.make_async_copy(
+            w_hbm.at[:, pl.ds(256 * n, 256)], weights.at[:, pl.ds(256 * n, 256)], local.at[2 + n]
+        )
+        for n in range(4)
+    ]
+    for load in loads + fetch:
+        load.start()
+    link.greet()
+
+    row = lax.broadcasted_iota(jnp.int32, (32, 128), 0)
+    first, second, half = row % 4, (row // 4) % 4, row // 16
+    ax = (link.x + jnp.where(half == 0, first, second)) % 4
+    ay = (link.y + jnp.where(half == 0, second, first)) % 4
+    block = (4 * ax + ay) * 2 + half
+    for dz, dk in LINE:
+        if (dz, dk) == (0, 0):
+            bias = jnp.zeros((32, 128), F32)
+        else:
+            base = 32 * (2 * ((link.z + dz) % 4) + (link.core + dk) % 2)
+            bias = jnp.full((32, 128), LOW, F32)
+            for i in range(ids_ref.shape[1]):
+                bias = jnp.where(block == ids_ref[0, i] - base, 0.0, bias)
+        outbox[slot(dz, dk), 0:32] = bias
+        outbox[slot(dz, dk), 32:40] = jnp.broadcast_to(weight_ref[...], (8, 128))
+
+    for load in loads:
+        load.wait()
+    link.meet()
+
+    shared = []
+    for zz in range(4):
+        give = pl.ds(pl.multiple_of((2 * zz + 1 - link.core) * 512, 512), 512)
+        shared.append(link.start(feats.at[:, give], other.at[:, pl.ds(512 * zz, 512)], dk=1))
+
+    for n in range(4):
+        fetch[n].wait()
+        unit[:, 256 * n : 256 * n + 256] = jnp.dot(
+            feats[...], weights[:, 256 * n : 256 * n + 256], preferred_element_type=F32
+        )
+    values = unit[...]
+    inverse[...] = lax.rsqrt(jnp.sum(values * values, axis=1, keepdims=True) + epsilon)
+    unit[...] = unit[...] * inverse[...]
 
     def q_rows(dz, dk, at=0, n=128):
         return queries.at[pl.ds(128 * slot(dz, dk) + at, n)]
@@ -105,23 +155,23 @@
 
     axes = (("dx", "dy"), ("dy", "dx"))
 
+    codes[0:64] = unit[128:192].astype(BF16)
+    codes[1024:1088] = unit[192:256].astype(BF16)
+    near = {}
+    for h in (0, 1):
+        a = axes[h][0]
+        near[h, 3] = link.start(code(h, 0, 0), code(h, 3, 0), **{a: 1})
+        near[h, 1] = link.start(code(h, 0, 0), code(h, 1, 0), **{a: -1})
+    queries[pl.ds(128 * OWN, 128)] = unit[0:128].astype(BF16)
+    q_in = {}
+    q_in[3] = link.start(q_rows(0, 0), q_rows(3, 0), dz=1)
+    q_in[1] = link.start(q_rows(0, 0), q_rows(1, 0), dz=-1)
+    s_in = {0: link.start(q_rows(0, 0), q_rows(0, 1), dk=1)}
     note_in = {}
     for dz, dk in PEERS:
         s, r = slot(dz, dk), slot(-dz, dk)
-        note_in[r] = link.start(note_ref.at[s], notes.at[r], dz=dz, dk=dk)
-    codes[0:64] = c_ref[0:64]
-    codes[1024:1088] = c_ref[64:128]
-    queries[pl.ds(128 * OWN, 128)] = q_ref[...]
-    notes[OWN] = note_ref[OWN]
-    near = {}
-    for h in (0, 1):
-        a = axes[h][0]
-        near[h, 3] = link.start(code(h, 0, 0), code(h, 3, 0), **{a: 1})
-        near[h, 1] = link.start(code(h, 0, 0), code(h, 1, 0), **{a: -1})
-    q_in = {}
-    q_in[3] = link.start(q_ref, q_rows(3, 0), dz=1)
-    q_in[1] = link.start(q_ref, q_rows(1, 0), dz=-1)
-    s_in = {0: link.start(q_ref, q_rows(0, 1), dk=1)}
+        note_in[r] = link.start(outbox.at[s], notes.at[r], dz=dz, dk=dk)
+    notes[OWN] = outbox[OWN]
 
     step = {}
 
@@ -141,26 +191,6 @@
         near[h, 3].wait_recv()
         far[h, 1] = link.start(code(h, 3, 0, 32, 32), code(h, 2, 0, 32, 32), **{a: 1})
         spread(h, 3)
-
-    moves, shared = [], []
-    for i, f_ref in enumerate((qf_ref, cf_ref)):
-        for zz in range(4):
-            keep = pl.ds(pl.multiple_of((2 * zz + link.core) * 512, 512), 512)
-            give = pl.ds(pl.multiple_of((2 * zz + 1 - link.core) * 512, 512), 512)
-            move = pltpu.make_async_copy(
-                f_ref.at[:, keep],
-                half_ref.at[pl.ds(128 * i, 128), pl.ds(512 * zz, 512)],
-                local.at[4 * i + zz],
-            )
-            move.start()
-            moves.append(move)
-            shared.append(
-                link.start(
-                    f_ref.at[:, give],
-                    half_ref.at[pl.ds(256 + 128 * i, 128), pl.ds(512 * zz, 512)],
-                    dk=1,
-                )
-            )
 
     top[...] = jnp.full(top.shape, LOW, F32)
     mass[...] = jnp.zeros(mass.shape, F32)
@@ -213,6 +243,13 @@
 
     onward(0)
     onward(1)
+    for copy in shared:
+        copy.wait_recv()
+    for zz in range(4):
+        keep = pl.ds(pl.multiple_of((2 * zz + link.core) * 512, 512), 512)
+        rows = slice(512 * zz, 512 * zz + 512)
+        turned[rows, 0:256] = feats[:, keep].T
+        turned[rows, 256:512] = other[:, rows].T
     q_far0.wait_recv()
     q_far1.wait_recv()
     s_in[2] = link.start(q_rows(2, 0), q_rows(2, 1), dk=1)
@@ -308,11 +345,13 @@
     home = {}
     for p, dz in enumerate((2, 1, 3, 0)):
         at = pl.ds(256 * p, 256)
-        lhs = grads[:, 256 * p : 256 * p + 256]
-
-        def product(n, carry, lhs=lhs, at=at):
+        turn[...] = grads[:, 256 * p : 256 * p + 256].T
+
+        def product(n, carry, at=at):
             cols = pl.ds(pl.multiple_of(256 * n, 256), 256)
-            dquery[at, cols] = dot_tn(lhs, codes[:, cols]).astype(BF16)
+            dquery[at, cols] = jnp.dot(
+                turn[...], codes[:, cols], preferred_element_type=F32
+            ).astype(BF16)
             return carry
 
         lax.fori_loop(0, width // 256, product, 0)
@@ -383,7 +422,7 @@
         + zp1[...].astype(F32)
         + zm1[...].astype(F32)
     )
-    dz_ref[0:128] = norm_back(d_q, qu_ref[...], qi_ref[...])
+    dz_ref[0:128] = norm_back(d_q, unit[0:128], inverse[0:128])
     pair_q = link.start(dz_ref.at[pl.ds(0, 128)], dz_ref.at[pl.ds(256, 128)], dk=1)
     outer(0)
     outer(1)
@@ -392,29 +431,10 @@
             back[h, name].wait_recv()
         s = slice(64 * h, 64 * h + 64)
         dc_sum[s] = dc_sum[s] + xp1[h].astype(F32) + xm1[h].astype(F32)
-    dz_ref[128:256] = norm_back(dc_sum[...], cu_ref[...], ci_ref[...])
+    dz_ref[128:256] = norm_back(dc_sum[...], unit[128:256], inverse[128:256])
     pair_c = link.start(dz_ref.at[pl.ds(128, 128)], dz_ref.at[pl.ds(384, 128)], dk=1)
     pair_q.wait_recv()
     pair_c.wait_recv()
-    for move in moves:
-        move.wait()
-    for copy in shared:
-        copy.wait_recv()
-    link.drain()
-
-
-N_ATTEND = 7 + 4 + 3 + 16 + 4 + 8 + 2 + 3 + 16 + 7 + 12 + 4 + 6 + 12 + 2
-
-
-PARTS = ((0, 384, "zxy"), (384, 384, "xyz"), (768, 256, "yzx"))
-
-
-def finish(dz_ref, half_ref, w_hbm, qg_ref, cg_ref, pg_ref, weights, partial, *rest):
-    boxes, (send, recv, local) = rest[:-3], rest[-3:]
-    link = Links(send, recv)
-    fetch = pltpu.make_async_copy(w_hbm, weights, local)
-    fetch.start()
-    link.barrier([{f"d{a}": s} for a in "xyz" for s in (1, -1)])
     here = {"x": link.x, "y": link.y, "z": link.z}
     per = len(boxes) // len(PARTS)
     rows_q = pg_ref.shape[0]
@@ -494,19 +514,19 @@
             self.level += 1
 
     parts = [Part(i) for i in range(len(PARTS))]
-    for part in (parts[2], parts[0], parts[1]):
+    for part in parts:
         cols = pl.ds(part.at, part.n)
 
         def product(i, carry, cols=cols, n=part.n):
             rows = pl.ds(pl.multiple_of(256 * i, 256), 256)
-            value = dot_tn(half_ref[:, rows], dz_ref[:, cols]).astype(BF16)
+            value = jnp.dot(
+                turned[rows], dz_ref[:, cols], preferred_element_type=F32
+            ).astype(BF16)
             partial[i // 2, pl.ds(2 * (i % 2), 2), :, :, cols] = value.reshape(2, 4, 32, n)
             return carry
 
         lax.fori_loop(0, 8, product, 0)
         part.open()
-
-    fetch.wait()
 
     def features(i, carry):
         rows = pl.ds(pl.multiple_of(256 * i, 256), 256)
@@ -515,7 +535,7 @@
         cg_ref[:, rows] = value[128:256]
         return carry
 
-    order = (parts[2], parts[0], parts[1])
+    order = parts
     lax.fori_loop(0, 8, features, 0)
     for part in order:
         part.relay()
@@ -533,57 +553,54 @@
     link.drain()
 
 
-def embed(features, projection):
-    values = jnp.dot(features, projection, preferred_element_type=F32)
-    inverse = lax.rsqrt(jnp.sum(values * values, axis=1, keepdims=True) + epsilon)
-    unit_vec = values * inverse
-    return (unit_vec, inverse, unit_vec.astype(BF16))
-
-
-def notes_of(hard_ids, loss_weight):
-    group, member = lax.axis_index("group"), lax.axis_index("member")
-    z, core, x, y = group // 2, group % 2, member // 4, member % 4
-    line = jnp.array(LINE, jnp.int32)
-    at = 2 * ((z + line[:, 0]) % 4) + (core + line[:, 1]) % 2
-    t = jnp.arange(8, dtype=jnp.int32)[:, None]
-    u = jnp.arange(4, dtype=jnp.int32)[None, :]
-    dx = jnp.where(t < 4, u, t - 4)
-    dy = jnp.where(t < 4, t, u)
-    block = ((4 * ((x + dx) % 4) + (y + dy) % 4) * 2 + t // 4).reshape(-1)
-    ids = at[:, None] * 32 + block[None, :]
-    wanted = jnp.any(ids[:, :, None] == hard_ids[0][None, None, :], axis=2)
-    wanted = wanted | (at == group)[:, None]
-    bias = jnp.where(wanted, 0.0, LOW).astype(F32)
-    bias = jnp.broadcast_to(bias[:, :, None], (8, 32, 128))
-    weight = jnp.broadcast_to(loss_weight[None, None, :], (8, 8, 128))
-    return jnp.concatenate([bias, weight], axis=1)
+def place(*refs):
+    n = len(refs) // 2
+    sems = refs[-1]
+    copies = [pltpu.make_async_copy(refs[i], refs[n + i], sems.at[i]) for i in range(n)]
+    for copy in copies:
+        copy.start()
+    for copy in copies:
+        copy.wait()
 
 
 def body(query_feat, code_feat, projection, hard_ids, loss_weight):
     rows, depth = query_feat.shape
     width = projection.shape[1]
-    q_unit, q_inv, q_emb = embed(query_feat, projection)
-    c_unit, c_inv, c_emb = embed(code_feat, projection)
-    notes = notes_of(hard_ids, loss_weight)
     vmem = pl.BlockSpec(memory_space=pltpu.VMEM)
     anywhere = pl.BlockSpec(memory_space=pl.ANY)
 
     def vm(*shape, dtype=BF16):
         return pltpu.VMEM(shape, dtype)
 
-    dz, half = pl.pallas_call(
-        attend,
-        out_shape=(
-            jax.ShapeDtypeStruct((4 * rows, width), BF16),
-            jax.ShapeDtypeStruct((4 * rows, depth // 2), BF16),
-        ),
-        in_specs=[vmem] * 7 + [anywhere] * 2,
-        out_specs=(vmem, anywhere),
+    boxes = []
+    for _, n, _ in PARTS:
+        for dims in ((4, 4), (4,), ()):
+            boxes += [vm(*dims, 16, n)] * 2 + [vm(*dims, 32, n)] * 3
+    outs = (
+        jax.ShapeDtypeStruct((rows, depth), BF16),
+        jax.ShapeDtypeStruct((rows, depth), BF16),
+        jax.ShapeDtypeStruct((depth // 128, width), F32),
+    )
+    made = pl.pallas_call(
+        step,
+        out_shape=outs,
+        in_specs=[anywhere] * 3 + [pl.BlockSpec(memory_space=pltpu.SMEM), vmem],
+        out_specs=(vmem, vmem, vmem),
         scratch_shapes=[
+            vm(8, 40, 128, dtype=F32),
+            vm(depth, width),
+            vm(4, 4, 4, 32, width),
+            vm(256, depth),
+            vm(256, depth // 2),
+            vm(depth // 2, 512),
+            vm(256, width, dtype=F32),
+            vm(256, 1, dtype=F32),
+            vm(512, width),
             vm(1024, width),
             vm(2048, width),
             vm(2048, 1024, dtype=F32),
             vm(2048, 1024),
+            vm(256, 2048),
             vm(2048, width),
             vm(1024, width),
             vm(8, 40, 128, dtype=F32),
@@ -609,41 +626,25 @@
             vm(256, width),
             vm(256, width),
             vm(128, width, dtype=F32),
-            pltpu.SemaphoreType.DMA((N_ATTEND,)),
-            pltpu.SemaphoreType.DMA((N_ATTEND,)),
-            pltpu.SemaphoreType.DMA((8,)),
+            *boxes,
+            pltpu.SemaphoreType.DMA((N_COPIES,)),
+            pltpu.SemaphoreType.DMA((N_COPIES,)),
+            pltpu.SemaphoreType.DMA((6,)),
         ],
         compiler_params=pltpu.CompilerParams(
-            collective_id=0, has_side_effects=True, vmem_limit_bytes=56 * 2**20
+            collective_id=0, has_side_effects=True, vmem_limit_bytes=60 * 2**20
         ),
-        name="attend",
-    )(q_emb, c_emb, notes, q_unit, q_inv, c_unit, c_inv, query_feat, code_feat)
-
-    boxes = []
-    for _, n, _ in PARTS:
-        for dims in ((4, 4), (4,), ()):
-            boxes += [vm(*dims, 16, n)] * 2 + [vm(*dims, 32, n)] * 3
+        name="step",
+    )(query_feat, code_feat, projection, hard_ids, loss_weight[None])
     return tuple(
         pl.pallas_call(
-            finish,
-            out_shape=(
-                jax.ShapeDtypeStruct((rows, depth), BF16),
-                jax.ShapeDtypeStruct((rows, depth), BF16),
-                jax.ShapeDtypeStruct((depth // 128, width), F32),
-            ),
-            in_specs=[vmem, vmem, anywhere],
-            out_specs=(vmem, vmem, vmem),
-            scratch_shapes=[vm(depth, width), vm(4, 4, 4, 32, width), *boxes]
-            + [
-                pltpu.SemaphoreType.DMA((54,)),
-                pltpu.SemaphoreType.DMA((54,)),
-                pltpu.SemaphoreType.DMA,
-            ],
-            compiler_params=pltpu.CompilerParams(
-                collective_id=1, has_side_effects=True, vmem_limit_bytes=56 * 2**20
-            ),
-            name="finish",
-        )(dz, half, projection)
+            place,
+            out_shape=outs,
+            in_specs=[vmem] * 3,
+            out_specs=(anywhere,) * 3,
+            scratch_shapes=[pltpu.SemaphoreType.DMA((3,))],
+            name="place",
+        )(*made)
     )
 
 

time: 150 us -> 128 us (0.85)
  matrix products: 9.77 us -> 0 us
  local copies, waits for them, and re-layouts: 8.7 us -> 0 us
  other arithmetic: 3.65 us -> 0 us
    dot_general x2 -> x0, matrix products: 9.77 us -> none  [embed(): values = jnp.dot(features, projection, preferred_element_type=F32)]
    unnamed x5 -> x0, local copies, waits for them, and re-layouts: 6.15 us -> none
where the time goes in v2:
time: 128 us; the launch traced here: 126 us
  Pallas kernels  126 us (98%)
    pallas_call x1, Pallas kernels, body(): pl.pallas_call(step, out_shape=outs, in_specs=[anywhere] * 3 + [pl.BlockS...  123 us
    pallas_call x1, Pallas kernels, body(): pl.pallas_call(place, out_shape=outs, in_specs=[vmem] * 3, out_specs=(any...  2.91 us

profile of v2, /device:TPU:1, one launch (start us, length us, event | category | flops | bytes accessed | tf_op | source)
XLA Modules:
  0.0 126.5 jit_solution(17243463493076542100)
XLA Ops:
  0.6 122.7 %step.1 = (bf16[128,4096]{1,0:T(8,128)(2,1)}, bf16[128,4096]{1,0:T(8,128)(2,1)}, f32[32,1024]{1,0:T(8,128)}) custom-call(bf16[128,4096]{1,0:T(8,128)(2,1)} %qf_hbm.1, bf16[128,4096]{1,0:T(8,128)(2,1)} %cf_hbm.1, bf16[4096,1024]{1,0:T(8,128)(2,1)} %w_hbm.1, s32[1,16]{1,0:T(1,128)} %ids_ref.1, f32[1,128]{1,0:T(1,128)} %bitcast.1), custom_call_target="tpu_custom_call" | custom-call | tf_op jit(solution)/shard_map/step/pallas_call | solution.py:584
  123.4 2.9 %place.1 = (bf16[128,4096]{1,0:T(8,128)(2,1)}, bf16[128,4096]{1,0:T(8,128)(2,1)}, f32[32,1024]{1,0:T(8,128)}) custom-call(bf16[128,4096]{1,0:T(8,128)(2,1)} %get-tuple-element.6.refs_0_, bf16[128,4096]{1,0:T(8,128)(2,1)} %get-tuple-element.7.refs_1_, f32[32,1024]{1,0:T(8,128)} %get-tuple-element.8.refs_2_), custom_call_target="tpu_custom_call" | custom-call | tf_op jit(solution)/shard_map/place/pallas_call | solution.py:640

commit v3 on v2

--- a/solution.py
+++ b/solution.py
@@ -85,14 +85,14 @@
 
 PARTS = ((0, 384, "zxy"), (384, 384, "xyz"), (768, 256, "yzx"))
 
-N_COPIES = 7 + 4 + 3 + 16 + 4 + 4 + 2 + 3 + 16 + 7 + 12 + 4 + 6 + 12 + 2 + 54
+N_COPIES = 7 + 4 + 3 + 16 + 4 + 4 + 2 + 3 + 16 + 7 + 12 + 4 + 6 + 12 + 2 + 36
 
 
 def step(
     qf_hbm, cf_hbm, w_hbm, ids_ref, weight_ref,
-    qg_ref, cg_ref, pg_ref,
-    outbox, weights, partial, feats, other, turned, unit, inverse, dz_ref,
-    queries, codes, scores, grads, turn, dcode, dquery, notes, mine, stats, top, mass, lse, scale,
+    qg_hbm, cg_hbm, pg_ref,
+    fgrads, outbox, bias_ref, weights, partial, feats, other, turned, unit, inverse, dz_ref,
+    queries, codes, scores, grads, turn, dcode, dquery, notes, mine, stats, top, mass, shift, scale,
     yp0, ym0, yp1, ym1, xp0, xm0, xp1, xm1, sib, zp0, zm0, zp1, zm1, low_a, low_b, dc_sum,
     *rest,
 ):
@@ -105,9 +105,9 @@
     ]
     fetch = [
         pltpu.make_async_copy(
-            w_hbm.at[:, pl.ds(256 * n, 256)], weights.at[:, pl.ds(256 * n, 256)], local.at[2 + n]
+            w_hbm.at[:, pl.ds(512 * n, 512)], weights.at[:, pl.ds(512 * n, 512)], local.at[2 + n]
         )
-        for n in range(4)
+        for n in range(2)
     ]
     for load in loads + fetch:
         load.start()
@@ -129,39 +129,46 @@
         outbox[slot(dz, dk), 0:32] = bias
         outbox[slot(dz, dk), 32:40] = jnp.broadcast_to(weight_ref[...], (8, 128))
 
-    for load in loads:
+    def embed(rows):
+        for n in range(2):
+            cols = slice(512 * n, 512 * n + 512)
+            unit[rows, cols] = jnp.dot(
+                feats[rows], weights[:, cols], preferred_element_type=F32
+            )
+        values = unit[rows]
+        inverse[rows] = lax.rsqrt(jnp.sum(values * values, axis=1, keepdims=True) + epsilon)
+        unit[rows] = unit[rows] * inverse[rows]
+
+    for load in loads + fetch:
         load.wait()
+    embed(slice(128, 256))
     link.meet()
-
-    shared = []
-    for zz in range(4):
-        give = pl.ds(pl.multiple_of((2 * zz + 1 - link.core) * 512, 512), 512)
-        shared.append(link.start(feats.at[:, give], other.at[:, pl.ds(512 * zz, 512)], dk=1))
-
-    for n in range(4):
-        fetch[n].wait()
-        unit[:, 256 * n : 256 * n + 256] = jnp.dot(
-            feats[...], weights[:, 256 * n : 256 * n + 256], preferred_element_type=F32
-        )
-    values = unit[...]
-    inverse[...] = lax.rsqrt(jnp.sum(values * values, axis=1, keepdims=True) + epsilon)
-    unit[...] = unit[...] * inverse[...]
 
     def q_rows(dz, dk, at=0, n=128):
         return queries.at[pl.ds(128 * slot(dz, dk) + at, n)]
 
     def code(half, first, second, at=0, n=64):
-        return codes.at[pl.ds(256 * (4 * half + second) + 64 * first + at, n)]
+        return codes.at[16 * half + 4 * second + first, pl.ds(at, n)]
 
     axes = (("dx", "dy"), ("dy", "dx"))
 
-    codes[0:64] = unit[128:192].astype(BF16)
-    codes[1024:1088] = unit[192:256].astype(BF16)
+    codes[0] = unit[128:192].astype(BF16)
+    codes[16] = unit[192:256].astype(BF16)
     near = {}
     for h in (0, 1):
         a = axes[h][0]
         near[h, 3] = link.start(code(h, 0, 0), code(h, 3, 0), **{a: 1})
         near[h, 1] = link.start(code(h, 0, 0), code(h, 1, 0), **{a: -1})
+    step = {}
+
+    def spread(h, f):
+        b = axes[h][1]
+        step[h, f, 3] = link.start(code(h, f, 0), code(h, f, 3), **{b: 1})
+        step[h, f, 1] = link.start(code(h, f, 0), code(h, f, 1), **{b: -1})
+
+    for h in (0, 1):
+        spread(h, 0)
+    embed(slice(0, 128))
     queries[pl.ds(128 * OWN, 128)] = unit[0:128].astype(BF16)
     q_in = {}
     q_in[3] = link.start(q_rows(0, 0), q_rows(3, 0), dz=1)
@@ -173,16 +180,12 @@
         note_in[r] = link.start(outbox.at[s], notes.at[r], dz=dz, dk=dk)
     notes[OWN] = outbox[OWN]
 
-    step = {}
-
-    def spread(h, f):
-        b = axes[h][1]
-        step[h, f, 3] = link.start(code(h, f, 0), code(h, f, 3), **{b: 1})
-        step[h, f, 1] = link.start(code(h, f, 0), code(h, f, 1), **{b: -1})
+    shared = []
+    for zz in range(4):
+        give = pl.ds(pl.multiple_of((2 * zz + 1 - link.core) * 512, 512), 512)
+        shared.append(link.start(feats.at[:, give], other.at[:, pl.ds(512 * zz, 512)], dk=1))
 
     far = {}
-    for h in (0, 1):
-        spread(h, 0)
     for h in (0, 1):
         a = axes[h][0]
         near[h, 1].wait_recv()
@@ -216,21 +219,16 @@
             step[h, f, 3].wait_recv()
             last[h, f, 1] = link.start(code(h, f, 3, 32, 32), code(h, f, 2, 32, 32), **{b: 1})
 
-    def score(t):
-        rows = pl.ds(256 * t, 256)
+    def score(h, f):
+        ids = [16 * h + 4 * s + f for s in range(4)]
+        lhs = jnp.concatenate([codes[i] for i in ids], axis=0)
+        s = inverse_temp * dot_nt(lhs, queries[...])
+        for u, i in enumerate(ids):
+            scores[i] = s[64 * u : 64 * u + 64] + bias_ref[i : i + 1]
 
         def part(j, carry):
             lanes = pl.ds(pl.multiple_of(256 * j, 256), 256)
-            s = inverse_temp * dot_nt(codes[rows], queries[pl.ds(pl.multiple_of(256 * j, 256), 256)])
-            pieces = []
-            for u in range(4):
-                bias = jnp.concatenate(
-                    [notes[2 * j, 4 * t + u : 4 * t + u + 1], notes[2 * j + 1, 4 * t + u : 4 * t + u + 1]],
-                    axis=1,
-                )
-                pieces.append(s[64 * u : 64 * u + 64] + bias)
-            s = jnp.concatenate(pieces, axis=0)
-            scores[rows, lanes] = s
+            s = jnp.concatenate([scores[i, :, lanes] for i in ids], axis=0)
             before = top[:, lanes]
             after = jnp.maximum(before, jnp.max(s, axis=0, keepdims=True))
             mass[:, lanes] = mass[:, lanes] * jnp.exp(before - after) + jnp.sum(
@@ -256,18 +254,17 @@
     onward(3)
     for copy in note_in.values():
         copy.wait_recv()
+    for s in range(8):
+        bias_ref[:, 128 * s : 128 * s + 128] = notes[s, 0:32]
     for dz in (0, 1, 3, 2):
         s_in[dz].wait_recv()
-    score(0)
-    score(4)
-    onward(2)
-    for t in (1, 3, 5, 7):
-        score(t)
-    for h in (0, 1):
-        for f in range(4):
+    for f in (0, 1, 3, 2):
+        if f == 1:
+            onward(2)
+        for h in (0, 1):
             last[h, f, 0].wait_recv()
             last[h, f, 1].wait_recv()
-        score(4 * h + 2)
+            score(h, f)
 
     for s in range(8):
         mine[s : s + 1] = top[:, 128 * s : 128 * s + 128]
@@ -283,17 +280,17 @@
         seen = [(slot(rz, rk), slot(tz - rz, tk + rk)) for rz, rk in LINE]
         most = functools.reduce(jnp.maximum, [stats[r, i : i + 1] for r, i in seen])
         whole = sum(stats[r, 8 + i : 9 + i] * jnp.exp(stats[r, i : i + 1] - most) for r, i in seen)
-        lse[:, 128 * t : 128 * t + 128] = most + jnp.log(whole)
-        scale[:, 128 * t : 128 * t + 128] = inverse_temp * notes[t, 32:33]
-
-    def backward(t):
+        factor = inverse_temp * notes[t, 32:33]
+        scale[:, 128 * t : 128 * t + 128] = factor
+        shift[:, 128 * t : 128 * t + 128] = most + jnp.log(whole) - jnp.log(factor)
+
+    def gradient(t):
         rows = pl.ds(256 * t, 256)
 
         def part(j, carry):
             lanes = pl.ds(pl.multiple_of(256 * j, 256), 256)
-            grads[rows, lanes] = (
-                scale[:, lanes] * jnp.exp(scores[rows, lanes] - lse[:, lanes])
-            ).astype(BF16)
+            s = scores[4 * t : 4 * t + 4, :, lanes].reshape(256, 256)
+            grads[rows, lanes] = jnp.exp(s - shift[:, lanes]).astype(BF16)
             return carry
 
         lax.fori_loop(0, 4, part, 0)
@@ -302,19 +299,20 @@
             own = slice(256 * t, 256 * t + 64)
             i = lax.broadcasted_iota(jnp.int32, (64, 128), 0) + 16 * t
             j = lax.broadcasted_iota(jnp.int32, (64, 128), 1)
-            hit = jnp.where(i == j, 1.0, 0.0).astype(F32)
+            hit = jnp.where(i == j, scale[:, lanes], 0.0)
             grads[own, lanes] = (
-                scale[:, lanes] * (jnp.exp(scores[own, lanes] - lse[:, lanes]) - hit)
+                jnp.exp(scores[4 * t, :, lanes] - shift[:, lanes]) - hit
             ).astype(BF16)
 
-        def product(n, carry):
-            cols = pl.ds(pl.multiple_of(256 * n, 256), 256)
-            dcode[rows, cols] = jnp.dot(
-                grads[rows, :], queries[:, cols], preferred_element_type=F32
-            ).astype(BF16)
-            return carry
-
-        lax.fori_loop(0, width // 256, product, 0)
+    def to_codes(t):
+        rows = pl.ds(256 * t, 256)
+        dcode[rows] = jnp.dot(
+            grads[rows], queries[...], preferred_element_type=F32
+        ).astype(BF16)
+
+    def backward(t):
+        gradient(t)
+        to_codes(t)
 
     def tile(h, t, at, n):
         return dcode.at[pl.ds(256 * (4 * h + t) + at, n)]
@@ -331,7 +329,7 @@
         back[h, "p1"] = link.start(tile(h, 1, 128, 128), yp1.at[h, pl.ds(128, 128)], **{b: 1})
         backward(4 * h + 3)
         back[h, "m1"] = link.start(tile(h, 3, 0, 128), ym1.at[h, pl.ds(0, 128)], **{b: -1})
-    for h in (0, 1):
+    def relay(h):
         b = axes[h][1]
         back[h, "p0"].wait_recv()
         add_into(tile(h, 1, 0, 128), tile(h, 1, 0, 128)[...], yp0[h])
@@ -339,37 +337,41 @@
         back[h, "m0"].wait_recv()
         add_into(tile(h, 3, 128, 128), tile(h, 3, 128, 128)[...], ym0[h])
         back[h, "m2"] = link.start(tile(h, 3, 128, 128), ym1.at[h, pl.ds(128, 128)], **{b: -1})
-    backward(0)
-    backward(4)
-
+
+    gradient(0)
+    gradient(4)
     home = {}
-    for p, dz in enumerate((2, 1, 3, 0)):
-        at = pl.ds(256 * p, 256)
+
+    def to_queries(dz):
+        p = PLACE[dz]
         turn[...] = grads[:, 256 * p : 256 * p + 256].T
-
-        def product(n, carry, at=at):
-            cols = pl.ds(pl.multiple_of(256 * n, 256), 256)
-            dquery[at, cols] = jnp.dot(
-                turn[...], codes[:, cols], preferred_element_type=F32
-            ).astype(BF16)
-            return carry
-
-        lax.fori_loop(0, width // 256, product, 0)
+        dquery[256 * p : 256 * p + 256] = jnp.dot(
+            turn[...], codes[...].reshape(2048, width), preferred_element_type=F32
+        ).astype(BF16)
         home[dz] = link.start(dquery.at[pl.ds(256 * p + 128, 128)], sib.at[p], dk=1)
 
     def dq(dz, at=0, n=128):
         return dquery.at[pl.ds(128 * slot(dz, 0) + at, n)]
 
-    for dz in (2, 1, 3):
+    def add_sibling(dz):
         home[dz].wait_recv()
         add_into(dq(dz), dq(dz)[...], sib[PLACE[dz]])
-        if dz == 2:
-            z0p = link.start(dq(2, 0, 64), zp0, dz=1)
-            z0m = link.start(dq(2, 64, 64), zm0, dz=-1)
-        elif dz == 1:
-            z1p = link.start(dq(1, 64, 64), zp1.at[pl.ds(64, 64)], dz=1)
-        else:
-            z1m = link.start(dq(3, 0, 64), zm1.at[pl.ds(0, 64)], dz=-1)
+
+    to_queries(2)
+    to_queries(1)
+    to_queries(3)
+    add_sibling(2)
+    z0p = link.start(dq(2, 0, 64), zp0, dz=1)
+    z0m = link.start(dq(2, 64, 64), zm0, dz=-1)
+    add_sibling(1)
+    z1p = link.start(dq(1, 64, 64), zp1.at[pl.ds(64, 64)], dz=1)
+    relay(0)
+    relay(1)
+    add_sibling(3)
+    z1m = link.start(dq(3, 0, 64), zm1.at[pl.ds(0, 64)], dz=-1)
+    to_queries(0)
+    to_codes(0)
+    to_codes(4)
 
     def inner(h):
         a = axes[h][0]
@@ -458,22 +460,32 @@
             return self.value.at[index + (rows,)]
 
         def box(self, name):
-            return self.boxes[5 * self.level + ("p0", "m0", "p1", "m1", "sum").index(name)]
+            if self.level == 0:
+                return self.boxes[("p0", "m0", "p1", "m1", "sum").index(name)]
+            return self.boxes[1 + 4 * self.level + ("p1", "m1", "far", "sum").index(name)]
 
         def rows_of(self, ref, rows):
             return ref.at[(slice(None),) * (len(self.left) - 1) + (rows,)]
 
-        def open(self):
+        def open(self, which=(2, 1, 3)):
             name = "d" + self.order[self.level]
-            self.c = {}
-            self.c["p0"] = link.start(self.chunk(2, low), self.box("p0"), **{name: 1})
-            self.c["m0"] = link.start(self.chunk(2, high), self.box("m0"), **{name: -1})
-            self.c["p1"] = link.start(
-                self.chunk(1, high), self.rows_of(self.box("p1"), high), **{name: 1}
-            )
-            self.c["m1"] = link.start(
-                self.chunk(3, low), self.rows_of(self.box("m1"), low), **{name: -1}
-            )
+            if 2 in which:
+                self.c = {}
+            if self.level:
+                for d, key in ((2, "far"), (1, "p1"), (3, "m1")):
+                    self.c[key] = link.start(self.chunk(d), self.box(key), **{name: d})
+                return
+            if 2 in which:
+                self.c["p0"] = link.start(self.chunk(2, low), self.box("p0"), **{name: 1})
+                self.c["m0"] = link.start(self.chunk(2, high), self.box("m0"), **{name: -1})
+            if 1 in which:
+                self.c["p1"] = link.start(
+                    self.chunk(1, high), self.rows_of(self.box("p1"), high), **{name: 1}
+                )
+            if 3 in which:
+                self.c["m1"] = link.start(
+                    self.chunk(3, low), self.rows_of(self.box("m1"), low), **{name: -1}
+                )
 
         def merge(self, dst, *terms):
             if len(dst.shape) <= 2:
@@ -500,9 +512,12 @@
             )
 
         def close(self):
-            for key in ("p1", "p2", "m1", "m2"):
-                self.c[key].wait_recv()
-            terms = (self.chunk(0), self.box("p1"), self.box("m1"))
+            for key, copy in self.c.items():
+                if key not in ("p0", "m0"):
+                    copy.wait_recv()
+            terms = [self.chunk(0), self.box("p1"), self.box("m1")]
+            if self.level:
+                terms.append(self.box("far"))
             if self.level == 2:
                 total = sum(t[...].astype(F32) for t in terms)
                 pg_ref[:, self.at : self.at + self.n] = total
@@ -514,42 +529,49 @@
             self.level += 1
 
     parts = [Part(i) for i in range(len(PARTS))]
-    for part in parts:
+    first = parts[0]
+    cols = pl.ds(first.at, first.n)
+    for d in (2, 1, 3, 0):
+        at = (link.z + d) % 4
+        rows = pl.ds(pl.multiple_of(512 * at, 512), 512)
+        value = jnp.dot(turned[rows], dz_ref[:, cols], preferred_element_type=F32)
+        partial[at, :, :, :, cols] = value.astype(BF16).reshape(4, 4, 32, first.n)
+        if d:
+            first.open((d,))
+    for part in parts[1:]:
         cols = pl.ds(part.at, part.n)
-
-        def product(i, carry, cols=cols, n=part.n):
-            rows = pl.ds(pl.multiple_of(256 * i, 256), 256)
-            value = jnp.dot(
-                turned[rows], dz_ref[:, cols], preferred_element_type=F32
-            ).astype(BF16)
-            partial[i // 2, pl.ds(2 * (i % 2), 2), :, :, cols] = value.reshape(2, 4, 32, n)
-            return carry
-
-        lax.fori_loop(0, 8, product, 0)
+        value = jnp.dot(turned[...], dz_ref[:, cols], preferred_element_type=F32)
+        partial[:, :, :, :, cols] = value.astype(BF16).reshape(4, 4, 4, 32, part.n)
         part.open()
 
-    def features(i, carry):
-        rows = pl.ds(pl.multiple_of(256 * i, 256), 256)
-        value = dot_nt(dz_ref[0:256], weights[rows]).astype(BF16)
-        qg_ref[:, rows] = value[0:128]
-        cg_ref[:, rows] = value[128:256]
-        return carry
-
-    order = parts
-    lax.fori_loop(0, 8, features, 0)
-    for part in order:
-        part.relay()
-    lax.fori_loop(8, 16, features, 0)
-    for part in order:
-        part.close()
-        part.open()
-    for level in (1, 2):
-        for part in order:
-            part.relay()
-        for part in order:
+    puts = []
+
+    def features(i):
+        rows = slice(1024 * i, 1024 * i + 1024)
+        fgrads[:, rows] = dot_nt(dz_ref[0:256], weights[rows]).astype(BF16)
+        for n, hbm in enumerate((qg_hbm, cg_hbm)):
+            put = pltpu.make_async_copy(
+                fgrads.at[pl.ds(128 * n, 128), pl.ds(1024 * i, 1024)],
+                hbm.at[:, pl.ds(1024 * i, 1024)],
+                local.at[4 + 2 * i + n],
+            )
+            put.start()
+            puts.append(put)
+
+    features(0)
+    features(1)
+    parts[0].relay()
+    features(2)
+    parts[1].relay()
+    parts[2].relay()
+    features(3)
+    for level in (0, 1, 2):
+        for part in parts:
             part.close()
-            if level == 1:
+            if level < 2:
                 part.open()
+    for put in puts:
+        put.wait()
     link.drain()
 
 
@@ -574,8 +596,8 @@
 
     boxes = []
     for _, n, _ in PARTS:
-        for dims in ((4, 4), (4,), ()):
-            boxes += [vm(*dims, 16, n)] * 2 + [vm(*dims, 32, n)] * 3
+        boxes += [vm(4, 4, 16, n)] * 2 + [vm(4, 4, 32, n)] * 3
+        boxes += [vm(4, 32, n)] * 4 + [vm(32, n)] * 4
     outs = (
         jax.ShapeDtypeStruct((rows, depth), BF16),
         jax.ShapeDtypeStruct((rows, depth), BF16),
@@ -585,9 +607,11 @@
         step,
         out_shape=outs,
         in_specs=[anywhere] * 3 + [pl.BlockSpec(memory_space=pltpu.SMEM), vmem],
-        out_specs=(vmem, vmem, vmem),
+        out_specs=(anywhere, anywhere, vmem),
         scratch_shapes=[
+            vm(256, depth),
             vm(8, 40, 128, dtype=F32),
+            vm(32, 1024, dtype=F32),
             vm(depth, width),
             vm(4, 4, 4, 32, width),
             vm(256, depth),
@@ -597,8 +621,8 @@
             vm(256, 1, dtype=F32),
             vm(512, width),
             vm(1024, width),
-            vm(2048, width),
-            vm(2048, 1024, dtype=F32),
+            vm(32, 64, width),
+            vm(32, 64, 1024, dtype=F32),
             vm(2048, 1024),
             vm(256, 2048),
             vm(2048, width),
@@ -629,7 +653,7 @@
             *boxes,
             pltpu.SemaphoreType.DMA((N_COPIES,)),
             pltpu.SemaphoreType.DMA((N_COPIES,)),
-            pltpu.SemaphoreType.DMA((6,)),
+            pltpu.SemaphoreType.DMA((12,)),
         ],
         compiler_params=pltpu.CompilerParams(
             collective_id=0, has_side_effects=True, vmem_limit_bytes=60 * 2**20

time: 128 us -> 112 us (0.88); the launches traced: 126 us -> 112 us
  Pallas kernels: 126 us -> 111 us
    pallas_call x1, Pallas kernels: 123 us -> 108 us  [body(): pl.pallas_call(step, out_shape=outs, in_specs=[anywhere] * 3 + [pl.BlockS...]
where the time goes in v3:
time: 112 us
  Pallas kernels  111 us (99%)
    pallas_call x1, Pallas kernels, body(): pl.pallas_call(step, out_shape=outs, in_specs=[anywhere] * 3 + [pl.BlockS...  108 us
    pallas_call x1, Pallas kernels, body(): pl.pallas_call(place, out_shape=outs, in_specs=[vmem] * 3, out_specs=(any...  2.91 us

profile of v3, /device:TPU:1, one launch (start us, length us, event | category | flops | bytes accessed | tf_op | source)
XLA Modules:
  0.0 111.9 jit_solution(3149276415010080702)
XLA Ops:
  0.6 108.2 %step.1 = (bf16[128,4096]{1,0:T(8,128)(2,1)}, bf16[128,4096]{1,0:T(8,128)(2,1)}, f32[32,1024]{1,0:T(8,128)}) custom-call(bf16[128,4096]{1,0:T(8,128)(2,1)} %qf_hbm.1, bf16[128,4096]{1,0:T(8,128)(2,1)} %cf_hbm.1, bf16[4096,1024]{1,0:T(8,128)(2,1)} %w_hbm.1, s32[1,16]{1,0:T(1,128)} %ids_ref.1, f32[1,128]{1,0:T(1,128)} %bitcast.1), custom_call_target="tpu_custom_call" | custom-call | tf_op jit(solution)/shard_map/step/pallas_call | solution.py:606
  108.8 2.9 %place.1 = (bf16[128,4096]{1,0:T(8,128)(2,1)}, bf16[128,4096]{1,0:T(8,128)(2,1)}, f32[32,1024]{1,0:T(8,128)}) custom-call(bf16[128,4096]{1,0:T(8,128)(2,1)} %get-tuple-element.6.refs_0_, bf16[128,4096]{1,0:T(8,128)(2,1)} %get-tuple-element.7.refs_1_, f32[32,1024]{1,0:T(8,128)} %get-tuple-element.8.refs_2_), custom_call_target="tpu_custom_call" | custom-call | tf_op jit(solution)/shard_map/place/pallas_call | solution.py:664

commit v4 on v3

--- a/solution.py
+++ b/solution.py
@@ -83,20 +83,28 @@
     return (inverse * (upstream - unit * inner)).astype(BF16)
 
 
-PARTS = ((0, 384, "zxy"), (384, 384, "xyz"), (768, 256, "yzx"))
-
-N_COPIES = 7 + 4 + 3 + 16 + 4 + 4 + 2 + 3 + 16 + 7 + 12 + 4 + 6 + 12 + 2 + 36
+PARTS = (
+    (0, 256, "zxy"),
+    (256, 128, "zxy"),
+    (384, 256, "xyz"),
+    (640, 128, "xyz"),
+    (768, 128, "yzx"),
+    (896, 128, "yzx"),
+)
+
+N_COPIES = 7 + 4 + 3 + 16 + 4 + 4 + 2 + 3 + 16 + 7 + 12 + 4 + 6 + 12 + 2 + 4 + 72
 
 
 def step(
     qf_hbm, cf_hbm, w_hbm, ids_ref, weight_ref,
     qg_hbm, cg_hbm, pg_ref,
-    fgrads, outbox, bias_ref, weights, partial, feats, other, turned, unit, inverse, dz_ref,
-    queries, codes, scores, grads, turn, dcode, dquery, notes, mine, stats, top, mass, shift, scale,
+    fgrads, outbox, bias_ref, weights, feats, other, turned, unit, inverse, dz_ref,
+    queries, codes, scores, grads, turn, dcode, dquery, notes, mine, mine_lse, stats, top, mass, shift, scale,
     yp0, ym0, yp1, ym1, xp0, xm0, xp1, xm1, sib, zp0, zm0, zp1, zm1, low_a, low_b, dc_sum,
     *rest,
 ):
     boxes, (send, recv, local) = rest[:-3], rest[-3:]
+    partial, boxes = boxes[: len(PARTS)], boxes[len(PARTS) :]
     width = weights.shape[1]
     link = Links(send, recv)
     loads = [
@@ -190,25 +198,13 @@
         a = axes[h][0]
         near[h, 1].wait_recv()
         far[h, 0] = link.start(code(h, 1, 0, 0, 32), code(h, 2, 0, 0, 32), **{a: -1})
-        spread(h, 1)
         near[h, 3].wait_recv()
         far[h, 1] = link.start(code(h, 3, 0, 32, 32), code(h, 2, 0, 32, 32), **{a: 1})
-        spread(h, 3)
+    for h in (0, 1):
+        spread(h, 1)
 
     top[...] = jnp.full(top.shape, LOW, F32)
     mass[...] = jnp.zeros(mass.shape, F32)
-
-    q_in[1].wait_recv()
-    q_far0 = link.start(q_rows(1, 0, 0, 64), q_rows(2, 0, 0, 64), dz=-1)
-    s_in[1] = link.start(q_rows(1, 0), q_rows(1, 1), dk=1)
-    q_in[3].wait_recv()
-    q_far1 = link.start(q_rows(3, 0, 64, 64), q_rows(2, 0, 64, 64), dz=1)
-    s_in[3] = link.start(q_rows(3, 0), q_rows(3, 1), dk=1)
-    for h in (0, 1):
-        far[h, 0].wait_recv()
-        far[h, 1].wait_recv()
-        spread(h, 2)
-
     last = {}
 
     def onward(f):
@@ -239,8 +235,24 @@
 
         lax.fori_loop(0, 4, part, 0)
 
+    for h in (0, 1):
+        far[h, 0].wait_recv()
+        far[h, 1].wait_recv()
+        spread(h, 2)
+    for h in (0, 1):
+        spread(h, 3)
+    q_in[1].wait_recv()
+    q_far0 = link.start(q_rows(1, 0, 0, 64), q_rows(2, 0, 0, 64), dz=-1)
+    s_in[1] = link.start(q_rows(1, 0), q_rows(1, 1), dk=1)
+    q_in[3].wait_recv()
+    q_far1 = link.start(q_rows(3, 0, 64, 64), q_rows(2, 0, 64, 64), dz=1)
+    s_in[3] = link.start(q_rows(3, 0), q_rows(3, 1), dk=1)
     onward(0)
     onward(1)
+    q_far0.wait_recv()
+    q_far1.wait_recv()
+    s_in[2] = link.start(q_rows(2, 0), q_rows(2, 1), dk=1)
+    onward(2)
     for copy in shared:
         copy.wait_recv()
     for zz in range(4):
@@ -248,41 +260,37 @@
         rows = slice(512 * zz, 512 * zz + 512)
         turned[rows, 0:256] = feats[:, keep].T
         turned[rows, 256:512] = other[:, rows].T
-    q_far0.wait_recv()
-    q_far1.wait_recv()
-    s_in[2] = link.start(q_rows(2, 0), q_rows(2, 1), dk=1)
-    onward(3)
     for copy in note_in.values():
         copy.wait_recv()
     for s in range(8):
         bias_ref[:, 128 * s : 128 * s + 128] = notes[s, 0:32]
+        scale[:, 128 * s : 128 * s + 128] = inverse_temp * notes[s, 32:33]
     for dz in (0, 1, 3, 2):
         s_in[dz].wait_recv()
-    for f in (0, 1, 3, 2):
+    for f in range(4):
         if f == 1:
-            onward(2)
+            onward(3)
         for h in (0, 1):
             last[h, f, 0].wait_recv()
             last[h, f, 1].wait_recv()
             score(h, f)
 
-    for s in range(8):
-        mine[s : s + 1] = top[:, 128 * s : 128 * s + 128]
-        mine[8 + s : 9 + s] = mass[:, 128 * s : 128 * s + 128]
+    groups = [(slot(dz, dk), link.device(dz=dz, dk=dk)[0]) for dz, dk in LINE]
+    for s, g in groups:
+        mine[0, pl.ds(g, 1)] = top[:, 128 * s : 128 * s + 128]
+        mine[1, pl.ds(g, 1)] = mass[:, 128 * s : 128 * s + 128]
     told = []
     for dz, dk in PEERS:
         told.append(link.start(mine, stats.at[slot(-dz, dk)], dz=dz, dk=dk))
     stats[OWN] = mine[...]
     for copy in told:
         copy.wait_recv()
-    for tz, tk in LINE:
-        t = slot(tz, tk)
-        seen = [(slot(rz, rk), slot(tz - rz, tk + rk)) for rz, rk in LINE]
-        most = functools.reduce(jnp.maximum, [stats[r, i : i + 1] for r, i in seen])
-        whole = sum(stats[r, 8 + i : 9 + i] * jnp.exp(stats[r, i : i + 1] - most) for r, i in seen)
-        factor = inverse_temp * notes[t, 32:33]
-        scale[:, 128 * t : 128 * t + 128] = factor
-        shift[:, 128 * t : 128 * t + 128] = most + jnp.log(whole) - jnp.log(factor)
+    most = functools.reduce(jnp.maximum, [stats[r, 0] for r in range(8)])
+    whole = sum(stats[r, 1] * jnp.exp(stats[r, 0] - most) for r in range(8))
+    mine_lse[...] = most + jnp.log(whole)
+    for s, g in groups:
+        lanes = slice(128 * s, 128 * s + 128)
+        shift[:, lanes] = mine_lse[pl.ds(g, 1)] - jnp.log(scale[:, lanes])
 
     def gradient(t):
         rows = pl.ds(256 * t, 256)
@@ -333,10 +341,13 @@
         b = axes[h][1]
         back[h, "p0"].wait_recv()
         add_into(tile(h, 1, 0, 128), tile(h, 1, 0, 128)[...], yp0[h])
-        back[h, "p2"] = link.start(tile(h, 1, 0, 128), yp1.at[h, pl.ds(0, 128)], **{b: 1})
         back[h, "m0"].wait_recv()
         add_into(tile(h, 3, 128, 128), tile(h, 3, 128, 128)[...], ym0[h])
-        back[h, "m2"] = link.start(tile(h, 3, 128, 128), ym1.at[h, pl.ds(128, 128)], **{b: -1})
+        for f in (1, 2, 0, 3):
+            t, to, way = (1, yp1, 1) if f < 2 else (3, ym1, -1)
+            back[h, "r", f] = link.start(
+                tile(h, t, 64 * f, 64), to.at[h, pl.ds(64 * f, 64)], **{b: way}
+            )
 
     gradient(0)
     gradient(4)
@@ -373,29 +384,30 @@
     to_codes(0)
     to_codes(4)
 
-    def inner(h):
+    def inner(h, f):
         a = axes[h][0]
-        for name in ("p1", "p2", "m1", "m2"):
-            back[h, name].wait_recv()
+        if f == 2:
+            for name in ("p1", "m1"):
+                back[h, name].wait_recv()
         low = (low_a, low_b)[h]
-        for f in (2, 1, 3, 0):
-            s = slice(64 * f, 64 * f + 64)
-            total = (
-                tile(h, 0, 64 * f, 64)[...].astype(F32)
-                + yp1[h, s].astype(F32)
-                + ym1[h, s].astype(F32)
-            )
-            if f == 0:
-                dc_sum[64 * h : 64 * h + 64] = total
-            else:
-                low[s] = total.astype(BF16)
-            if f == 2:
-                back[h, "q0"] = link.start(low.at[pl.ds(128, 32)], xp0.at[h], **{a: 1})
-                back[h, "n0"] = link.start(low.at[pl.ds(160, 32)], xm0.at[h], **{a: -1})
-            if f == 1:
-                back[h, "q1"] = link.start(low.at[pl.ds(96, 32)], xp1.at[h, pl.ds(32, 32)], **{a: 1})
-            if f == 3:
-                back[h, "n1"] = link.start(low.at[pl.ds(192, 32)], xm1.at[h, pl.ds(0, 32)], **{a: -1})
+        back[h, "r", f].wait_recv()
+        s = slice(64 * f, 64 * f + 64)
+        total = (
+            tile(h, 0, 64 * f, 64)[...].astype(F32)
+            + yp1[h, s].astype(F32)
+            + ym1[h, s].astype(F32)
+        )
+        if f == 0:
+            dc_sum[64 * h : 64 * h + 64] = total
+        else:
+            low[s] = total.astype(BF16)
+        if f == 2:
+            back[h, "q0"] = link.start(low.at[pl.ds(128, 32)], xp0.at[h], **{a: 1})
+            back[h, "n0"] = link.start(low.at[pl.ds(160, 32)], xm0.at[h], **{a: -1})
+        if f == 1:
+            back[h, "q1"] = link.start(low.at[pl.ds(96, 32)], xp1.at[h, pl.ds(32, 32)], **{a: 1})
+        if f == 3:
+            back[h, "n1"] = link.start(low.at[pl.ds(192, 32)], xm1.at[h, pl.ds(0, 32)], **{a: -1})
 
     def outer(h):
         a = axes[h][0]
@@ -413,8 +425,11 @@
     z0m.wait_recv()
     add_into(dq(3, 64, 64), dq(3, 64, 64)[...], zm0[...])
     z2m = link.start(dq(3, 64, 64), zm1.at[pl.ds(64, 64)], dz=-1)
-    inner(0)
-    inner(1)
+    for f in (2, 1, 3, 0):
+        for h in (0, 1):
+            inner(h, f)
+    outer(0)
+    outer(1)
     home[0].wait_recv()
     for copy in (z1p, z2p, z1m, z2m):
         copy.wait_recv()
@@ -426,8 +441,6 @@
     )
     dz_ref[0:128] = norm_back(d_q, unit[0:128], inverse[0:128])
     pair_q = link.start(dz_ref.at[pl.ds(0, 128)], dz_ref.at[pl.ds(256, 128)], dk=1)
-    outer(0)
-    outer(1)
     for h in (0, 1):
         for name in ("q1", "q2", "n1", "n2"):
             back[h, name].wait_recv()
@@ -439,8 +452,7 @@
     pair_c.wait_recv()
     here = {"x": link.x, "y": link.y, "z": link.z}
     per = len(boxes) // len(PARTS)
-    rows_q = pg_ref.shape[0]
-    low, high = pl.ds(0, rows_q // 2), pl.ds(rows_q // 2, rows_q // 2)
+    low, high = pl.ds(0, 2), pl.ds(2, 2)
 
     class Part:
         def __init__(self, i):
@@ -448,24 +460,25 @@
             self.boxes = boxes[per * i : per * i + per]
             self.left = "zxy"
             self.level = 0
-            self.value = None
-
-        def chunk(self, d, rows=slice(None)):
+            self.value = partial[i]
+
+        def chunk(self, d, half=slice(None)):
             axis = self.order[self.level]
-            index = tuple(
-                (here[a] + d) % 4 if a == axis else slice(None) for a in self.left
-            )
-            if self.level == 0:
-                return partial.at[index + (rows, pl.ds(self.at, self.n))]
-            return self.value.at[index + (rows,)]
+            index, rest = [], [half]
+            for a in self.left:
+                if a == axis:
+                    index.append((here[a] + d) % 4)
+                else:
+                    index.append(rest.pop() if rest else slice(None))
+            return self.value.at[tuple(index)]
 
         def box(self, name):
             if self.level == 0:
                 return self.boxes[("p0", "m0", "p1", "m1", "sum").index(name)]
             return self.boxes[1 + 4 * self.level + ("p1", "m1", "far", "sum").index(name)]
 
-        def rows_of(self, ref, rows):
-            return ref.at[(slice(None),) * (len(self.left) - 1) + (rows,)]
+        def rows_of(self, ref, half):
+            return ref.at[half]
 
         def open(self, which=(2, 1, 3)):
             name = "d" + self.order[self.level]
@@ -529,20 +542,24 @@
             self.level += 1
 
     parts = [Part(i) for i in range(len(PARTS))]
-    first = parts[0]
-    cols = pl.ds(first.at, first.n)
     for d in (2, 1, 3, 0):
         at = (link.z + d) % 4
         rows = pl.ds(pl.multiple_of(512 * at, 512), 512)
-        value = jnp.dot(turned[rows], dz_ref[:, cols], preferred_element_type=F32)
-        partial[at, :, :, :, cols] = value.astype(BF16).reshape(4, 4, 32, first.n)
+        value = jnp.dot(turned[rows], dz_ref[:, 0:384], preferred_element_type=F32)
+        value = value.astype(BF16).reshape(4, 4, 32, 384)
+        partial[0][at] = value[:, :, :, 0:256]
+        partial[1][at] = value[:, :, :, 256:384]
         if d:
-            first.open((d,))
-    for part in parts[1:]:
-        cols = pl.ds(part.at, part.n)
-        value = jnp.dot(turned[...], dz_ref[:, cols], preferred_element_type=F32)
-        partial[:, :, :, :, cols] = value.astype(BF16).reshape(4, 4, 4, 32, part.n)
-        part.open()
+            parts[0].open((d,))
+    parts[1].open((2,))
+    for i in (2, 4):
+        at, n = parts[i].at, parts[i].n + parts[i + 1].n
+        value = jnp.dot(turned[...], dz_ref[:, at : at + n], preferred_element_type=F32)
+        value = value.astype(BF16).reshape(4, 4, 4, 32, n)
+        partial[i][...] = value[..., 0 : parts[i].n]
+        partial[i + 1][...] = value[..., parts[i].n :]
+        parts[i].open()
+        parts[i + 1].open((2,))
 
     puts = []
 
@@ -559,14 +576,17 @@
             puts.append(put)
 
     features(0)
-    features(1)
-    parts[0].relay()
-    features(2)
-    parts[1].relay()
-    parts[2].relay()
+    for i in (0, 4, 2):
+        parts[i].relay()
+        parts[i + 1].open((1, 3))
+        if i != 2:
+            features(1 + i // 4)
+    for i in (1, 5, 3):
+        parts[i].relay()
     features(3)
-    for level in (0, 1, 2):
-        for part in parts:
+    order = [parts[i] for i in (4, 0, 2, 5, 1, 3)]
+    for level in range(3):
+        for part in order:
             part.close()
             if level < 2:
                 part.open()
@@ -575,13 +595,21 @@
     link.drain()
 
 
-def place(*refs):
-    n = len(refs) // 2
-    sems = refs[-1]
-    copies = [pltpu.make_async_copy(refs[i], refs[n + i], sems.at[i]) for i in range(n)]
-    for copy in copies:
+def place(q_in, c_in, p_in, q_out, c_out, p_out, q_held, c_held, p_held, come, leave):
+    width = q_held.shape[1] // 4
+    pairs = [(p_in, p_held, p_out)]
+    for i in range(4):
+        cols = pl.ds(width * i, width)
+        pairs.append((q_in.at[:, cols], q_held.at[:, cols], q_out.at[:, cols]))
+        pairs.append((c_in.at[:, cols], c_held.at[:, cols], c_out.at[:, cols]))
+    first = [pltpu.make_async_copy(a, b, come.at[i]) for i, (a, b, _) in enumerate(pairs)]
+    second = [pltpu.make_async_copy(b, c, leave.at[i]) for i, (_, b, c) in enumerate(pairs)]
+    for copy in first:
         copy.start()
-    for copy in copies:
+    for copy, onward in zip(first, second):
+        copy.wait()
+        onward.start()
+    for copy in second:
         copy.wait()
 
 
@@ -596,7 +624,7 @@
 
     boxes = []
     for _, n, _ in PARTS:
-        boxes += [vm(4, 4, 16, n)] * 2 + [vm(4, 4, 32, n)] * 3
+        boxes += [vm(2, 4, 32, n)] * 2 + [vm(4, 4, 32, n)] * 3
         boxes += [vm(4, 32, n)] * 4 + [vm(32, n)] * 4
     outs = (
         jax.ShapeDtypeStruct((rows, depth), BF16),
@@ -613,7 +641,6 @@
             vm(8, 40, 128, dtype=F32),
             vm(32, 1024, dtype=F32),
             vm(depth, width),
-            vm(4, 4, 4, 32, width),
             vm(256, depth),
             vm(256, depth // 2),
             vm(depth // 2, 512),
@@ -628,8 +655,9 @@
             vm(2048, width),
             vm(1024, width),
             vm(8, 40, 128, dtype=F32),
-            vm(16, 128, dtype=F32),
-            vm(8, 16, 128, dtype=F32),
+            vm(2, 8, 128, dtype=F32),
+            vm(8, 128, dtype=F32),
+            vm(8, 2, 8, 128, dtype=F32),
             vm(1, 1024, dtype=F32),
             vm(1, 1024, dtype=F32),
             vm(1, 1024, dtype=F32),
@@ -650,6 +678,7 @@
             vm(256, width),
             vm(256, width),
             vm(128, width, dtype=F32),
+            *[vm(4, 4, 4, 32, n) for _, n, _ in PARTS],
             *boxes,
             pltpu.SemaphoreType.DMA((N_COPIES,)),
             pltpu.SemaphoreType.DMA((N_COPIES,)),
@@ -664,9 +693,15 @@
         pl.pallas_call(
             place,
             out_shape=outs,
-            in_specs=[vmem] * 3,
+            in_specs=[anywhere] * 3,
             out_specs=(anywhere,) * 3,
-            scratch_shapes=[pltpu.SemaphoreType.DMA((3,))],
+            scratch_shapes=[
+                vm(rows, depth),
+                vm(rows, depth),
+                vm(depth // 128, width, dtype=F32),
+                pltpu.SemaphoreType.DMA((9,)),
+                pltpu.SemaphoreType.DMA((9,)),
+            ],
             name="place",
         )(*made)
     )

time: 112 us -> 106 us (0.946)
  Pallas kernels: 111 us -> 105 us
    pallas_call x1, Pallas kernels: 108 us -> 103 us  [body(): pl.pallas_call(step, out_shape=outs, in_specs=[anywhere] * 3 + [pl.BlockS...]
where the time goes in v4:
time: 106 us
  Pallas kernels  105 us (99%)
    pallas_call x1, Pallas kernels, body(): pl.pallas_call(step, out_shape=outs, in_specs=[anywhere] * 3 + [pl.BlockS...  103 us
    pallas_call x1, Pallas kernels, body(): pl.pallas_call(place, out_shape=outs, in_specs=[anywhere] * 3, out_specs=...  2.48 us

profile of v4, /device:TPU:1, one launch (start us, length us, event | category | flops | bytes accessed | tf_op | source)
XLA Modules:
  0.0 106.2 jit_solution(9908387368952337107)
XLA Ops:
  0.6 102.9 %step.1 = (bf16[128,4096]{1,0:T(8,128)(2,1)}, bf16[128,4096]{1,0:T(8,128)(2,1)}, f32[32,1024]{1,0:T(8,128)}) custom-call(bf16[128,4096]{1,0:T(8,128)(2,1)} %qf_hbm.1, bf16[128,4096]{1,0:T(8,128)(2,1)} %cf_hbm.1, bf16[4096,1024]{1,0:T(8,128)(2,1)} %w_hbm.1, s32[1,16]{1,0:T(1,128)} %ids_ref.1, f32[1,128]{1,0:T(1,128)} %bitcast.1), custom_call_target="tpu_custom_call" | custom-call | tf_op jit(solution)/shard_map/step/pallas_call | solution.py:634
  103.5 2.5 %place.1 = (bf16[128,4096]{1,0:T(8,128)(2,1)}, bf16[128,4096]{1,0:T(8,128)(2,1)}, f32[32,1024]{1,0:T(8,128)}) custom-call(bf16[128,4096]{1,0:T(8,128)(2,1)} %get-tuple-element.6.q_in, bf16[128,4096]{1,0:T(8,128)(2,1)} %get-tuple-element.7.c_in, f32[32,1024]{1,0:T(8,128)} %get-tuple-element.8.p_in), custom_call_target="tpu_custom_call" | custom-call | tf_op jit(solution)/shard_map/place/pallas_call | solution.py:693

commit v5 on v4

--- a/solution.py
+++ b/solution.py
@@ -28,7 +28,7 @@
 
 class Links:
     def __init__(self, send, recv):
-        self.send, self.recv, self.made = send, recv, []
+        self.send, self.recv, self.made, self.left = send, recv, [], 0
         group, member = lax.axis_index("group"), lax.axis_index("member")
         self.z, self.core = group // 2, group % 2
         self.x, self.y = member // 4, member % 4
@@ -62,9 +62,11 @@
     def meet(self):
         pl.semaphore_wait(pltpu.get_barrier_semaphore(), 4 + len(PEERS))
 
-    def drain(self):
-        for copy in self.made:
+    def drain(self, upto=None):
+        upto = len(self.made) if upto is None else upto
+        for copy in self.made[self.left : upto]:
             copy.wait_send()
+        self.left = upto
 
 
 def dot_nt(a, b):
@@ -117,7 +119,7 @@
         )
         for n in range(2)
     ]
-    for load in loads + fetch:
+    for load in (loads[1], *fetch, loads[0]):
         load.start()
     link.greet()
 
@@ -137,8 +139,10 @@
         outbox[slot(dz, dk), 0:32] = bias
         outbox[slot(dz, dk), 32:40] = jnp.broadcast_to(weight_ref[...], (8, 128))
 
-    def embed(rows):
+    def embed(rows, waits=()):
         for n in range(2):
+            if waits:
+                waits[n].wait()
             cols = slice(512 * n, 512 * n + 512)
             unit[rows, cols] = jnp.dot(
                 feats[rows], weights[:, cols], preferred_element_type=F32
@@ -147,9 +151,9 @@
         inverse[rows] = lax.rsqrt(jnp.sum(values * values, axis=1, keepdims=True) + epsilon)
         unit[rows] = unit[rows] * inverse[rows]
 
-    for load in loads + fetch:
-        load.wait()
-    embed(slice(128, 256))
+    loads[1].wait()
+    embed(slice(128, 256), fetch)
+    loads[0].wait()
     link.meet()
 
     def q_rows(dz, dk, at=0, n=128):
@@ -215,8 +219,7 @@
             step[h, f, 3].wait_recv()
             last[h, f, 1] = link.start(code(h, f, 3, 32, 32), code(h, f, 2, 32, 32), **{b: 1})
 
-    def score(h, f):
-        ids = [16 * h + 4 * s + f for s in range(4)]
+    def score(ids):
         lhs = jnp.concatenate([codes[i] for i in ids], axis=0)
         s = inverse_temp * dot_nt(lhs, queries[...])
         for u, i in enumerate(ids):
@@ -267,13 +270,23 @@
         scale[:, 128 * s : 128 * s + 128] = inverse_temp * notes[s, 32:33]
     for dz in (0, 1, 3, 2):
         s_in[dz].wait_recv()
-    for f in range(4):
+    def blocks(h, f, seconds=(0, 1, 2, 3)):
+        return [16 * h + 4 * s + f for s in seconds]
+
+    def finish_row(h, f):
+        last[h, f, 0].wait_recv()
+        last[h, f, 1].wait_recv()
+
+    for f in range(3):
         if f == 1:
             onward(3)
         for h in (0, 1):
-            last[h, f, 0].wait_recv()
-            last[h, f, 1].wait_recv()
-            score(h, f)
+            finish_row(h, f)
+            score(blocks(h, f))
+    score(blocks(0, 3, (0, 1, 3)) + blocks(1, 3, (0, 1, 3)))
+    finish_row(0, 3)
+    finish_row(1, 3)
+    score(blocks(0, 3, (2,)) + blocks(1, 3, (2,)))
 
     groups = [(slot(dz, dk), link.device(dz=dz, dk=dk)[0]) for dz, dk in LINE]
     for s, g in groups:
@@ -370,17 +383,17 @@
 
     to_queries(2)
     to_queries(1)
-    to_queries(3)
+    relay(0)
+    relay(1)
     add_sibling(2)
     z0p = link.start(dq(2, 0, 64), zp0, dz=1)
     z0m = link.start(dq(2, 64, 64), zm0, dz=-1)
     add_sibling(1)
     z1p = link.start(dq(1, 64, 64), zp1.at[pl.ds(64, 64)], dz=1)
-    relay(0)
-    relay(1)
+    to_queries(3)
+    to_queries(0)
     add_sibling(3)
     z1m = link.start(dq(3, 0, 64), zm1.at[pl.ds(0, 64)], dz=-1)
-    to_queries(0)
     to_codes(0)
     to_codes(4)
 
@@ -542,6 +555,7 @@
             self.level += 1
 
     parts = [Part(i) for i in range(len(PARTS))]
+    before = len(link.made)
     for d in (2, 1, 3, 0):
         at = (link.z + d) % 4
         rows = pl.ds(pl.multiple_of(512 * at, 512), 512)
@@ -576,6 +590,7 @@
             puts.append(put)
 
     features(0)
+    link.drain(before)
     for i in (0, 4, 2):
         parts[i].relay()
         parts[i + 1].open((1, 3))
@@ -586,6 +601,8 @@
     features(3)
     order = [parts[i] for i in (4, 0, 2, 5, 1, 3)]
     for level in range(3):
+        link.drain(before)
+        before = len(link.made)
         for part in order:
             part.close()
             if level < 2:

time: 106 us -> 106 us (level)
  no operation moved by 1% of the time
where the time goes in v5:
time: 106 us; the launch traced here: 105 us
  Pallas kernels  105 us (99%)
    pallas_call x1, Pallas kernels, body(): pl.pallas_call(step, out_shape=outs, in_specs=[anywhere] * 3 + [pl.BlockS...  102 us
    pallas_call x1, Pallas kernels, body(): pl.pallas_call(place, out_shape=outs, in_specs=[anywhere] * 3, out_specs=...  2.48 us

profile of v5, /device:TPU:1, one launch (start us, length us, event | category | flops | bytes accessed | tf_op | source)
XLA Modules:
  0.0 105.4 jit_solution(2941705052195556988)
XLA Ops:
  0.6 102.2 %step.1 = (bf16[128,4096]{1,0:T(8,128)(2,1)}, bf16[128,4096]{1,0:T(8,128)(2,1)}, f32[32,1024]{1,0:T(8,128)}) custom-call(bf16[128,4096]{1,0:T(8,128)(2,1)} %qf_hbm.1, bf16[128,4096]{1,0:T(8,128)(2,1)} %cf_hbm.1, bf16[4096,1024]{1,0:T(8,128)(2,1)} %w_hbm.1, s32[1,16]{1,0:T(1,128)} %ids_ref.1, f32[1,128]{1,0:T(1,128)} %bitcast.1), custom_call_target="tpu_custom_call" | custom-call | tf_op jit(solution)/shard_map/step/pallas_call | solution.py:651
  102.8 2.5 %place.1 = (bf16[128,4096]{1,0:T(8,128)(2,1)}, bf16[128,4096]{1,0:T(8,128)(2,1)}, f32[32,1024]{1,0:T(8,128)}) custom-call(bf16[128,4096]{1,0:T(8,128)(2,1)} %get-tuple-element.6.q_in, bf16[128,4096]{1,0:T(8,128)(2,1)} %get-tuple-element.7.c_in, f32[32,1024]{1,0:T(8,128)} %get-tuple-element.8.p_in), custom_call_target="tpu_custom_call" | custom-call | tf_op jit(solution)/shard_map/place/pallas_call | solution.py:710
